TPU v7x, 256 devices: a whole 4x4x8 slice. The times are simulated.
256 devices in a mesh: stretch: 4 (over z_lo, core), seq: 64 (over x, y, z_hi).
Axes of the slice: x: 4, y: 4, z: 8 (z_hi: 4, z_lo: 2; z = z_hi * 2 + z_lo), core: 2. Of those that a mesh axis runs over, the one named last changes fastest.
Arguments:
- queries: bfloat16 [4, 3072, 4096], P('stretch', 'seq'), may hold values from -30 to 30
- keys: bfloat16 [4, 3072, 4096], P('stretch', 'seq'), may hold values from -30 to 30
- values: bfloat16 [4, 3072, 4096], P('stretch', 'seq'), may hold values from -6 to 6
- levels: int32 [4], replicated, may hold values from 0 to 63
- gate_table: float32 [64, 4096], replicated, may hold values from 0.25 to 2
Outputs:
- blended: bfloat16 [4, 3072, 4096], P('stretch', 'seq')
All inputs are finite; a program needn't handle non-finite values.
Results may differ from a plain program's by a relative error of at most 0.0095.
Values may be sent and summed in bfloat16 or wider, within the bound.
No kernel may reach another device: no remote copies, remote signals or barrier semaphores. Data moves between devices by JAX's collectives and lax.ppermute only.
A program may use at most 64 MiB of HBM per device.

v0:
```python
from functools import partial
import math

import jax
import jax.numpy as jnp
from jax import lax
from jax.sharding import PartitionSpec as P

H = 32
DH = 128


def unchanged(softmax_state):
    return softmax_state


def local(queries, keys, values, levels, gate_table):
    seq_count = lax.axis_size("seq")
    stretch_count = lax.axis_size("stretch")
    groups = min(H, seq_count)
    query_parts = seq_count // groups
    group_width = H * DH // groups
    per_group = H // groups
    tokens = queries.shape[1]
    token_share = tokens // query_parts
    stretch_span = seq_count * tokens
    key_block_len = 512
    own_stretch = lax.axis_index("stretch")
    score_scale = 1.0 / math.sqrt(DH)
    query_send = queries[0].reshape(query_parts, token_share, groups, group_width)
    query_send = query_send.transpose(2, 0, 1, 3).reshape(seq_count, token_share, group_width)
    query_recv = lax.all_to_all(query_send, "seq", split_axis=0, concat_axis=0, tiled=True)
    query_rows = query_recv.reshape(seq_count * token_share, per_group, DH)

    def spread(array):
        leading = array.shape[0]
        array = array.reshape(leading, tokens, groups, group_width).transpose(0, 2, 1, 3)
        array = jnp.broadcast_to(
            array[:, :, None], (leading, groups, query_parts, tokens, group_width)
        )
        return array.reshape(leading, seq_count, tokens, group_width)

    def absorb(softmax_state, query_block, key_stretch, value_stretch):
        key_blocks = key_stretch.reshape(
            stretch_span // key_block_len, key_block_len, per_group, DH
        )
        value_blocks = value_stretch.reshape(
            stretch_span // key_block_len, key_block_len, per_group, DH
        )

        def absorb_block(running, block_pair):
            running_peak, running_total, accumulated = running
            key_block, value_block = block_pair
            scores = (
                jnp.einsum(
                    "qhd,khd->hqk", query_block, key_block, preferred_element_type=jnp.float32
                )
                * score_scale
            )
            new_peak = jnp.maximum(running_peak, jnp.max(scores, axis=2))
            shrink = jnp.exp(running_peak - new_peak)
            weights = jnp.exp(scores - new_peak[:, :, None])
            running_total = running_total * shrink + jnp.sum(weights, axis=2)
            mixture = jnp.einsum(
                "hqk,khd->qhd",
                weights.astype(jnp.bfloat16),
                value_block,
                preferred_element_type=jnp.float32,
            )
            accumulated = accumulated * shrink.T[:, :, None] + mixture
            return ((new_peak, running_total, accumulated), None)

        softmax_state, _ = lax.scan(absorb_block, softmax_state, (key_blocks, value_blocks))
        return softmax_state

    def start_state(query_block):
        count_rows = query_block.shape[0]
        return (
            jnp.full((per_group, count_rows), -1e30, jnp.float32),
            jnp.zeros((per_group, count_rows), jnp.float32),
            jnp.zeros((count_rows, per_group, DH), jnp.float32),
        )

    batches = [(query_rows, own_stretch)]
    initial = tuple((start_state(entry[0]) for entry in batches))
    all_keys, all_values = (
        lax.all_gather(keys, "stretch", axis=0, tiled=True),
        lax.all_gather(values, "stretch", axis=0, tiled=True),
    )
    head_keys, head_values = (
        lax.all_to_all(spread(all_keys), "seq", split_axis=1, concat_axis=1, tiled=True),
        lax.all_to_all(spread(all_values), "seq", split_axis=1, concat_axis=1, tiled=True),
    )
    states = initial
    for stretch_index in range(stretch_count):
        visit_key_stretch = head_keys[stretch_index].reshape(stretch_span, per_group, DH)
        visit_value_stretch = head_values[stretch_index].reshape(stretch_span, per_group, DH)
        updated = []
        for (visit_query_block, stretch_limit), visit_softmax_state in zip(batches, states):
            taken = partial(
                absorb,
                query_block=visit_query_block,
                key_stretch=visit_key_stretch,
                value_stretch=visit_value_stretch,
            )
            updated.append(
                lax.cond(stretch_index <= stretch_limit, taken, unchanged, visit_softmax_state)
            )
        states = tuple(updated)
    finished = []
    for running_peak, running_total, accumulated in states:
        normalized = accumulated / running_total.T[:, :, None]
        finished.append(normalized.astype(jnp.bfloat16).reshape(normalized.shape[0], group_width))
    mixture = finished[0]
    result_send = mixture.reshape(seq_count, token_share, group_width)
    result_recv = lax.all_to_all(result_send, "seq", split_axis=0, concat_axis=0, tiled=True)
    attended = result_recv.reshape(groups, query_parts, token_share, group_width)
    attended = attended.transpose(1, 2, 0, 3).reshape(tokens, H * DH)
    gate_row = gate_table[levels[own_stretch]]
    blended = (gate_row[None, :] * attended.astype(jnp.float32)).astype(jnp.bfloat16)
    return blended[None]


def solution(mesh):
    placed = (
        P("stretch", "seq", None),
        P("stretch", "seq", None),
        P("stretch", "seq", None),
        P(),
        P(),
    )
    return jax.shard_map(
        local, mesh=mesh, in_specs=placed, out_specs=P("stretch", "seq", None), check_vma=False
    )
```

profile of v0, /device:TPU:33, one launch (start us, length us, event | category | flops | bytes accessed | tf_op | source)
XLA Modules:
  0.0 434.3 jit_solution(1044364987541614093)
XLA Ops:
  7.3 31.1 %all-gather.3.cloned.1.call-done = bf16[4,48,4096]{2,1,0:T(8,128)(2,1)} async-done(((bf16[1,48,4096]{2,1,0:T(8,128)(2,1)}), bf16[4,48,4096]{2,1,0:T(8,128)(2,1)}) %all-gather.3.cloned.1.call-update) | async-done | bytes 1572880 | tf_op jit(solution)/shard_map/all_gather | solution.py:87
  38.3 1.7 copy.57
  41.0 2.6 broadcast_in_dim.24
  43.6 13.1 %all-to-all-start = ((bf16[4,64,48,128]{3,2,0,1:T(8,128)(2,1)}), bf16[4,64,48,128]{3,2,0,1:T(8,128)(2,1)}, u32[]{:S(2)}, u32[]{:S(2)}) async-start(bf16[4,64,48,128]{3,2,0,1:T(8,128)(2,1)} %bitcast.179), calls=%async_computation | async-start | bytes 6291456 | tf_op jit(solution)/shard_map/all_to_all | solution.py:91
  57.5 65.4 %all-gather.5.cloned.1.call-done = bf16[4,48,4096]{2,1,0:T(8,128)(2,1)} async-done(((bf16[1,48,4096]{2,1,0:T(8,128)(2,1)}), bf16[4,48,4096]{2,1,0:T(8,128)(2,1)}) %all-gather.5.cloned.1.call-update) | async-done | bytes 1572880 | tf_op jit(solution)/shard_map/all_gather | solution.py:88
  122.9 1.7 copy.58
  125.6 18.4 %all-to-all-done = bf16[4,64,48,128]{3,2,0,1:T(8,128)(2,1)} async-done(((bf16[4,64,48,128]{3,2,0,1:T(8,128)(2,1)}), bf16[4,64,48,128]{3,2,0,1:T(8,128)(2,1)}, u32[]{:S(2)}, u32[]{:S(2)}) %all-to-all-start) | async-done | bytes 3145760 | tf_op jit(solution)/shard_map/all_to_all | solution.py:91
  144.0 2.6 broadcast_in_dim.26
  146.7 5.7 %all-to-all-start.1 = ((bf16[4,64,48,128]{3,2,0,1:T(8,128)(2,1)}), bf16[4,64,48,128]{3,2,0,1:T(8,128)(2,1)}, u32[]{:S(2)}, u32[]{:S(2)}) async-start(bf16[4,64,48,128]{3,2,0,1:T(8,128)(2,1)} %bitcast.180), calls=%async_computation.1 | async-start | bytes 6291456 | tf_op jit(solution)/shard_map/all_to_all | solution.py:92
  153.4 56.4 %all-to-all-done.1 = bf16[4,64,48,128]{3,2,0,1:T(8,128)(2,1)} async-done(((bf16[4,64,48,128]{3,2,0,1:T(8,128)(2,1)}), bf16[4,64,48,128]{3,2,0,1:T(8,128)(2,1)}, u32[]{:S(2)}, u32[]{:S(2)}) %all-to-all-start.1) | async-done | bytes 3145760 | tf_op jit(solution)/shard_map/all_to_all | solution.py:92
  209.8 6.5 %all-to-all-start.2 = ((bf16[64,24,128]{2,1,0:T(8,128)(2,1)}), bf16[64,24,128]{2,1,0:T(8,128)(2,1)S(1)}, u32[]{:S(2)}, u32[]{:S(2)}) async-start(bf16[64,24,128]{2,1,0:T(8,128)(2,1)} %bitcast.42), calls=%async_computation.2 | async-start | bytes 786432 | tf_op jit(solution)/shard_map/all_to_all | solution.py:32
  216.3 2.4 fusion.59
  218.7 2.4 fusion.58
  221.0 13.5 %all-to-all-done.2 = bf16[64,24,128]{2,1,0:T(8,128)(2,1)S(1)} async-done(((bf16[64,24,128]{2,1,0:T(8,128)(2,1)}), bf16[64,24,128]{2,1,0:T(8,128)(2,1)S(1)}, u32[]{:S(2)}, u32[]{:S(2)}) %all-to-all-start.2) | async-done | bytes 393248 | tf_op jit(solution)/shard_map/all_to_all | solution.py:32
  234.5 43.1 %conditional.4 = (f32[1,1536]{1,0:T(1,128)}, f32[1,1536]{1,0:T(1,128)}, f32[1536,1,128]{0,2,1:T(8,128)}) conditional(s32[]{:T(128)} %convert_element_type.67, () %tuple.48, (bf16[1,64,48,128]{3,2,0,1:T(8,128)(2,1)}, bf16[1,64,48,128]{3,2,0,1:T(8,128)(2,1)}, bf16[1536,1,128]{2,0,1:T(8,128)(2,1)S(1)}) %tuple.166), branch_computations={%region_0.0_spmd, %region_1.6_spmd} | conditional | flops 407970816 | bytes 11770081 | solution.py:107
  234.5 43.1 %while.56 = (s32[]{:T(128)}, f32[1,1536]{1,0:T(1,128)}, f32[1,1536]{1,0:T(1,128)}, f32[1536,1,128]{0,2,1:T(8,128)}, bf16[6,512,1,128]{3,1,2,0:T(8,128)(2,1)}, /*...) while((s32[]{:T(128)}, f32[1,1536]{1,0:T(1,128)}, ...), condition=%wide.region_5.5_spmd.clone, body=%wide.region_2.4_spmd.clone.sunk | while | flops 407970816 | bytes 11769977 | solution.py:73
  234.5 1.5 fusion.105
  237.8 2.5 fusion.109
  240.3 1.5 fusion.105
  243.0 1.3 fusion.108
  244.9 2.8 fusion.109
  247.7 1.5 fusion.105
  250.5 1.3 fusion.108
  252.4 2.8 fusion.109
  255.2 1.5 fusion.105
  257.9 1.3 fusion.108
  259.9 2.8 fusion.109
  262.7 1.5 fusion.105
  265.4 1.3 fusion.108
  267.3 2.8 fusion.109
  270.1 1.5 fusion.105
  272.9 1.3 fusion.108
  274.8 2.8 fusion.109
  277.6 38.8 %conditional.5 = ((f32[1,1536]{1,0:T(1,128)}, f32[1,1536]{1,0:T(1,128)}, f32[1536,1,128]{0,2,1:T(8,128)})) conditional(s32[]{:T(128)} %convert_element_type.66, (f32[1,1536]{1,0:T(1,128)}, f32[1,1536]{1,0:T(1,128)}, f32[1536,1,128]{0,2,1:T(8,128)}) %conditional.4, (bf16[1,64,48,128]{3,2,0,1:T(8,128)(2,1)S(1)}, ...), branch_computations={%region_6.7_spmd, %region_7.12_spmd} | conditional | flops 407769600 | bytes 11774157 | solution.py:107
  277.6 38.8 %while.53 = (s32[]{:T(128)}, f32[1,1536]{1,0:T(1,128)}, f32[1,1536]{1,0:T(1,128)}, f32[1536,1,128]{0,2,1:T(8,128)}, bf16[6,512,1,128]{3,1,2,0:T(8,128)(2,1)S(1)}...) while((s32[]{:T(128)}, f32[1,1536]{1,0:T(1,128)}, ...), condition=%wide.region_11.11_spmd, body=%wide.region_8.10_spmd.sunk | while | flops 407769600 | bytes 11774053 | solution.py:73
  281.3 2.8 fusion.102
  287.8 2.8 fusion.102
  294.3 2.8 fusion.102
  300.7 2.8 fusion.102
  307.2 2.8 fusion.102
  313.7 2.8 fusion.102
  316.4 43.8 %conditional.6 = ((f32[1,1536]{1,0:T(1,128)}, f32[1,1536]{1,0:T(1,128)}, f32[1536,1,128]{0,2,1:T(8,128)})) conditional(s32[]{:T(128)} %convert_element_type.65, (f32[1,1536]{1,0:T(1,128)}, f32[1,1536]{1,0:T(1,128)}, f32[1536,1,128]{0,2,1:T(8,128)}) %get-tuple-element.810, (bf16[4,64,48,128]{3,2,0,1:T(8,128)(2,1)}, ...), branch_computations={%region_12.13_spmd, %region_13.18_spmd} | conditional | flops 407769600 | bytes 27502796 | solution.py:107
  316.4 2.4 copy.49
  318.9 2.4 copy.50
  321.4 38.8 %while.54 = (s32[]{:T(128)}, f32[1,1536]{1,0:T(1,128)}, f32[1,1536]{1,0:T(1,128)}, f32[1536,1,128]{0,2,1:T(8,128)}, bf16[6,512,1,128]{3,1,2,0:T(8,128)(2,1)S(1)}...) while((s32[]{:T(128)}, f32[1,1536]{1,0:T(1,128)}, ...), condition=%wide.region_17.17_spmd, body=%wide.region_14.16_spmd.sunk | while | flops 407769600 | bytes 11774053 | solution.py:73
  325.1 2.8 fusion.96
  331.6 2.8 fusion.96
  338.1 2.8 fusion.96
  344.5 2.8 fusion.96
  351.0 2.8 fusion.96
  357.5 2.8 fusion.96
  360.2 45.2 %conditional.7 = (f32[1,1536]{1,0:T(1,128)}, f32[1536,1,128]{2,0,1:T(8,128)S(1)}) conditional(s32[]{:T(128)} %convert_element_type.64, (f32[1,1536]{1,0:T(1,128)}, f32[1536,1,128]{0,2,1:T(8,128)}) %tuple.52, (bf16[4,64,48,128]{3,2,0,1:T(8,128)(2,1)}, bf16[4,64,48,128]{3,2,0,1:T(8,128)(2,1)}, bf16[1536,1,128]{2,0,1:T(8,128)(2,1)S(1)}, ...), branch_computations={%region_18.19_spmd, %region_19.24_spmd} | conditional | flops 407769600 | bytes 29075644 | solution.py:107
  360.2 2.4 copy.51
  362.7 2.4 copy.52
  365.2 38.8 %while.55 = (s32[]{:T(128)}, f32[1,1536]{1,0:T(1,128)}, f32[1,1536]{1,0:T(1,128)}, f32[1536,1,128]{0,2,1:T(8,128)}, bf16[6,512,1,128]{3,1,2,0:T(8,128)(2,1)S(1)}...) while((s32[]{:T(128)}, f32[1,1536]{1,0:T(1,128)}, ...), condition=%wide.region_23.23_spmd, body=%wide.region_20.22_spmd.sunk | while | flops 407769600 | bytes 11774053 | solution.py:73
  369.0 2.8 fusion.90
  375.4 2.8 fusion.90
  381.9 2.8 fusion.90
  388.4 2.8 fusion.90
  394.8 2.8 fusion.90
  401.3 2.8 fusion.90
  404.1 1.4 copy.56
  407.2 5.5 %all-to-all-start.3 = ((bf16[64,24,128]{2,1,0:T(8,128)(2,1)}), bf16[64,24,128]{2,1,0:T(8,128)(2,1)S(1)}, u32[]{:S(2)}, u32[]{:S(2)}) async-start(bf16[64,24,128]{2,1,0:T(8,128)(2,1)} %bitcast.44), calls=%async_computation.3 | async-start | bytes 786432 | tf_op jit(solution)/shard_map/all_to_all | solution.py:116
  415.5 10.7 %all-to-all-done.3 = bf16[64,24,128]{2,1,0:T(8,128)(2,1)S(1)} async-done(((bf16[64,24,128]{2,1,0:T(8,128)(2,1)}), bf16[64,24,128]{2,1,0:T(8,128)(2,1)S(1)}, u32[]{:S(2)}, u32[]{:S(2)}) %all-to-all-start.3) | async-done | bytes 393248 | tf_op jit(solution)/shard_map/all_to_all | solution.py:116
  (140 shorter events, 85.7 us)
Async XLA Ops:
  6.5 408.9 %copy-start = (f32[64,4096]{1,0:T(8,128)S(1)}, f32[64,4096]{1,0:T(8,128)}, u32[]{:S(2)}) copy-start(f32[64,4096]{1,0:T(8,128)} %param.25) | copy-start | bytes 3145732
  6.5 31.8 %all-gather.3.cloned.1.call-start = ((), (), s32[]{:S(2)}) async-start(), calls=%async_computation.4 | async-start | bytes 1966080 | tf_op jit(solution)/shard_map/all_gather | solution.py:87
  43.6 100.4 %all-to-all-start = ((bf16[4,64,48,128]{3,2,0,1:T(8,128)(2,1)}), bf16[4,64,48,128]{3,2,0,1:T(8,128)(2,1)}, u32[]{:S(2)}, u32[]{:S(2)}) async-start(bf16[4,64,48,128]{3,2,0,1:T(8,128)(2,1)} %bitcast.179), calls=%async_computation | async-start | bytes 6291456 | tf_op jit(solution)/shard_map/all_to_all | solution.py:91
  56.7 66.2 %all-gather.5.cloned.1.call-start = ((), (), s32[]{:S(2)}) async-start(), calls=%async_computation.5 | async-start | bytes 1966080 | tf_op jit(solution)/shard_map/all_gather | solution.py:88
  146.7 5.7 %copy-start.1 = (bf16[1,48,4096]{2,1,0:T(8,128)(2,1)S(1)}, bf16[1,48,4096]{2,1,0:T(8,128)(2,1)}, u32[]{:S(2)}) copy-start(bf16[1,48,4096]{2,1,0:T(8,128)(2,1)} %param.21) | copy-start | bytes 1179652
  146.7 63.1 %all-to-all-start.1 = ((bf16[4,64,48,128]{3,2,0,1:T(8,128)(2,1)}), bf16[4,64,48,128]{3,2,0,1:T(8,128)(2,1)}, u32[]{:S(2)}, u32[]{:S(2)}) async-start(bf16[4,64,48,128]{3,2,0,1:T(8,128)(2,1)} %bitcast.180), calls=%async_computation.1 | async-start | bytes 6291456 | tf_op jit(solution)/shard_map/all_to_all | solution.py:92
  209.8 24.7 %all-to-all-start.2 = ((bf16[64,24,128]{2,1,0:T(8,128)(2,1)}), bf16[64,24,128]{2,1,0:T(8,128)(2,1)S(1)}, u32[]{:S(2)}, u32[]{:S(2)}) async-start(bf16[64,24,128]{2,1,0:T(8,128)(2,1)} %bitcast.42), calls=%async_computation.2 | async-start | bytes 786432 | tf_op jit(solution)/shard_map/all_to_all | solution.py:32
  360.2 52.5 %copy-start.2 = (s32[4]{0:T(128)S(1)}, s32[4]{0:T(128)}, u32[]{:S(2)}) copy-start(s32[4]{0:T(128)} %param.24) | copy-start | bytes 52
  407.2 19.0 %all-to-all-start.3 = ((bf16[64,24,128]{2,1,0:T(8,128)(2,1)}), bf16[64,24,128]{2,1,0:T(8,128)(2,1)S(1)}, u32[]{:S(2)}, u32[]{:S(2)}) async-start(bf16[64,24,128]{2,1,0:T(8,128)(2,1)} %bitcast.44), calls=%async_computation.3 | async-start | bytes 786432 | tf_op jit(solution)/shard_map/all_to_all | solution.py:116
Sparse Core Ops, SparseCore 0:
  9.2 29.1 all-gather.2
  59.4 63.5 all-gather.4
where the time goes:
time: 438 us; the launch traced here: 434 us
  waiting for transfers between devices  197 us (45%)
  matrix products  85.4 us (19%)
  other arithmetic  62.2 us (14%)
  local copies, waits for them, and re-layouts  42.9 us (10%)
  starting transfers between devices  30.8 us (7%)
  between operations  15.6 us (4%)
    dot_general x24, matrix products, absorb_block(): jnp.einsum('hqk,khd->qhd', weights.astype(jnp.bfloat16), value_block, pre...  66.2 us
    all_gather x1, waiting for transfers between devices, local(): lax.all_gather(values, 'stretch', axis=0, tiled=True)  65.4 us
    all_to_all x1, waiting for transfers between devices, local(): lax.all_to_all(spread(all_values), 'seq', split_axis=1, concat_axis=1, ti...  56.4 us
    all_gather x1, waiting for transfers between devices, local(): lax.all_gather(keys, 'stretch', axis=0, tiled=True)  31.1 us
    add x24, other arithmetic, absorb_block(): running_total = running_total * shrink + jnp.sum(weights, axis=2)  31 us
    dot_general x24, matrix products, absorb_block(): jnp.einsum('qhd,khd->hqk', query_block, key_block, preferred_element_type...  19.3 us
    all_to_all x1, waiting for transfers between devices, local(): lax.all_to_all(spread(all_keys), 'seq', split_axis=1, concat_axis=1, tile...  18.4 us
    exp x24, other arithmetic, absorb_block(): shrink = jnp.exp(running_peak - new_peak)  17 us
  transfers between devices with their start and end apart: 6, of which 6 were waited for; matrix products, arithmetic and copies ran while one was open for 2% of the time, Pallas kernels for 0%

commit v1 on v0

v1 whole, which is shorter than its diff:
```python
from functools import partial
import math

import jax
import jax.numpy as jnp
from jax import lax
from jax.experimental import pallas as pl
from jax.experimental.pallas import tpu as pltpu
from jax.sharding import PartitionSpec as P

H = 32
DH = 128
AXES = ("stretch", "seq")
SCALE = math.log2(math.e) / math.sqrt(DH)
ROWS = 512
KEYS = 512
VMEM = 56 * 2**20


def exchange(flip_stretch, flip_seq, keep=lambda stretch: True):
    return [
        (c * 64 + s, (c ^ flip_stretch) * 64 + (s ^ flip_seq))
        for c in range(4)
        for s in range(64)
        if keep(c)
    ]


def send(array, pairs):
    return lax.ppermute(array, AXES, pairs)


def softmax_blocks(q, blocks):
    peak = total = mixture = None
    for load_key, load_value in blocks:
        scores = (
            lax.dot_general(
                q, load_key(), (((1,), (1,)), ((), ())), preferred_element_type=jnp.float32
            )
            * SCALE
        )
        block_peak = jnp.max(scores, axis=1, keepdims=True)
        new_peak = block_peak if peak is None else jnp.maximum(peak, block_peak)
        weights = jnp.exp2(scores - new_peak)
        value = load_value()
        value = jnp.concatenate([value, jnp.ones_like(value)], axis=1)
        part = jnp.dot(weights.astype(jnp.bfloat16), value, preferred_element_type=jnp.float32)
        if peak is not None:
            part = mixture * jnp.exp2(peak - new_peak) + part
        mixture, peak = part, new_peak
    total = mixture[:, DH:]
    return mixture[:, :DH] / total, peak + jnp.log2(total)


def loaders(pick, span):
    return [
        (partial(pick, 0, slice(at, at + KEYS)), partial(pick, 1, slice(at, at + KEYS)))
        for at in range(0, span, KEYS)
    ]


def store(mixture_ref, level_ref, mixture, level):
    mixture_ref[...] = mixture.astype(mixture_ref.dtype)
    level_ref[...] = level.T[:8]


def own_kernel(q_ref, near_ref, far_ref, mixture_ref, level_ref):
    blocks = []
    for ref in (near_ref, far_ref):
        blocks += loaders(lambda which, at, ref=ref: ref[which, at, :], ref.shape[1])
    store(mixture_ref, level_ref, *softmax_blocks(q_ref[...], blocks))


def pair_kernel(
    where_ref, q_ref, q_core_ref, x_ref, core_ref, mixture_ref, level_ref
):
    first = where_ref[1] == 0
    q = jnp.where(first, q_core_ref[...], q_ref[...])

    def pick(which, at):
        return jnp.where(first, x_ref[which, at, :], core_ref[which, at, :])

    store(mixture_ref, level_ref, *softmax_blocks(q, loaders(pick, x_ref.shape[1])))


def chip_kernel(
    where_ref, q_ref, z_ref, zv_ref, zc_ref, x_ref, xc_ref, mixture_ref, level_ref
):
    even = where_ref[0] == 0
    here = pl.ds(pl.program_id(0) * ROWS, ROWS)
    q = jnp.where(even, z_ref[here, :], q_ref[...])

    def pick(which, at):
        z = (z_ref, zv_ref)[which][at, :]
        return jnp.where(even, x_ref[which, at, :], z)

    def pick_core(which, at):
        return jnp.where(even, xc_ref[which, at, :], zc_ref[which, at, :])

    span = x_ref.shape[1]
    store(
        mixture_ref,
        level_ref,
        *softmax_blocks(q, loaders(pick, span) + loaders(pick_core, span)),
    )


def merge_kernel(where_ref, gate_ref, own, own_l, pair, pair_l, pair_in, pair_in_l, chip, chip_l, chip_in, chip_in_l, out_ref):
    odd = where_ref[0] == 1
    second = where_ref[1] == 1
    parts = [(own, own_l, None)]
    parts += [(pair, pair_l, second), (pair_in, pair_in_l, second)]
    parts += [(chip, chip_l, odd), (chip_in, chip_in_l, odd)]
    levels = []
    for _, level_ref, use in parts:
        level = jnp.broadcast_to(level_ref[0:1, :], (DH, level_ref.shape[1]))
        if use is not None:
            level = jnp.where(use, level, -jnp.inf)
        levels.append(level)
    top = levels[0]
    for level in levels[1:]:
        top = jnp.maximum(top, level)
    weights = [jnp.exp2(level - top) for level in levels]
    total = sum(weights[1:], weights[0])
    mixture = 0.0
    for (ref, _, use), weight in zip(parts, weights):
        part = ref[...].astype(jnp.float32) * (weight / total).T
        if use is not None:
            part = jnp.where(use, part, 0.0)
        mixture += part
    attended = mixture.astype(jnp.bfloat16).astype(jnp.float32)
    out_ref[...] = (gate_ref[...] * attended).astype(jnp.bfloat16)


def run(kernel, name, scalars, rows_in, whole_in, span, keys_seen):
    def rows(ndim):
        return pl.BlockSpec((ROWS, DH), lambda i, *_: (i, 0))

    in_specs = [rows(a.ndim) for a in rows_in]
    in_specs += [
        pl.BlockSpec(a.shape, lambda i, *_, n=a.ndim: (0,) * n) for a in whole_in
    ]
    return pl.pallas_call(
        kernel,
        grid_spec=pltpu.PrefetchScalarGridSpec(
            num_scalar_prefetch=len(scalars),
            grid=(span // ROWS,),
            in_specs=in_specs,
            out_specs=[rows(2), pl.BlockSpec((8, ROWS), lambda i, *_: (0, i))],
        ),
        out_shape=[
            jax.ShapeDtypeStruct((span, DH), jnp.bfloat16),
            jax.ShapeDtypeStruct((8, span), jnp.float32),
        ],
        compiler_params=pltpu.CompilerParams(vmem_limit_bytes=VMEM),
        cost_estimate=pl.CostEstimate(
            flops=8 * span * keys_seen * DH, bytes_accessed=0, transcendentals=span * keys_seen
        ),
        name=name,
    )(*scalars, *rows_in, *whole_in)


def merge(where, gate, parts, span):
    specs = []
    for _ in range(len(parts) // 2):
        specs.append(pl.BlockSpec((ROWS, DH), lambda i, *_: (i, 0)))
        specs.append(pl.BlockSpec((8, ROWS), lambda i, *_: (0, i)))
    return pl.pallas_call(
        merge_kernel,
        grid_spec=pltpu.PrefetchScalarGridSpec(
            num_scalar_prefetch=1,
            grid=(span // ROWS,),
            in_specs=[pl.BlockSpec((1, DH), lambda i, *_: (0, 0))] + specs,
            out_specs=pl.BlockSpec((ROWS, DH), lambda i, *_: (i, 0)),
        ),
        out_shape=jax.ShapeDtypeStruct((span, DH), jnp.bfloat16),
        compiler_params=pltpu.CompilerParams(vmem_limit_bytes=VMEM),
        name="merge",
    )(where, gate, *parts)


def local(queries, keys, values, levels, gate_table):
    tokens = queries.shape[1]
    half = tokens // 2
    span = 64 * half
    stretch = lax.axis_index("stretch")
    seq = lax.axis_index("seq")
    where = jnp.stack([stretch // 2, stretch % 2]).astype(jnp.int32)
    head = 16 * (seq // 32) + seq % 16
    gate = lax.dynamic_slice(gate_table, (levels[stretch], head * DH), (1, DH))

    qkv = jnp.concatenate([queries, keys, values])
    qkv = qkv.reshape(3, 2, half, 2, 16, DH).transpose(3, 1, 4, 0, 2, 5)
    qkv = lax.all_to_all(qkv.reshape(64, 3, half, DH), "seq", 0, 0, tiled=True)
    qkv = qkv.transpose(1, 0, 2, 3).reshape(3, span, DH)
    q, kv = qkv[0], qkv[1:]

    core = exchange(1, 0)
    kv_x = send(kv, exchange(0, 16))
    z = send(jnp.where(where[0] == 0, kv[0], q), exchange(2, 0))
    zv = send(kv[1], exchange(2, 0, lambda stretch: stretch < 2))
    kv_c = send(kv, core)
    q_c = send(q, core)
    kv_xc = send(kv_x, core)
    zc = send(jnp.stack([z, zv]), core)

    chip = run(chip_kernel, "chip", [where], [q], [z, zv, zc, kv_x, kv_xc], span, 2 * span)
    chip_in = [send(a, exchange(2, 0, lambda stretch: stretch < 2)) for a in chip]
    pair = run(pair_kernel, "pair", [where], [q, q_c], [kv_x, kv_c], span, span)
    pair_in = [send(a, exchange(1, 0, lambda stretch: stretch % 2 == 0)) for a in pair]
    own = run(own_kernel, "own", [], [q], [kv, kv_x], span, 2 * span)
    mixture = merge(where, gate, [*own, *pair, *pair_in, *chip, *chip_in], span)

    result = lax.all_to_all(mixture.reshape(64, half, DH), "seq", 0, 0, tiled=True)
    result = result.reshape(2, 2, 16, half, DH).transpose(1, 3, 0, 2, 4)
    return result.reshape(1, tokens, H * DH)


def solution(mesh):
    placed = (
        P("stretch", "seq", None),
        P("stretch", "seq", None),
        P("stretch", "seq", None),
        P(),
        P(),
    )
    return jax.shard_map(
        local, mesh=mesh, in_specs=placed, out_specs=P("stretch", "seq", None), check_vma=False
    )
```

time: 438 us -> 139 us (0.32)
  the two profiles are of different devices: /device:TPU:33 before, /device:TPU:32 now
where the time goes in v1:
time: 139 us; the launch traced here: 138 us
  waiting for transfers between devices  49.7 us (36%)
  Pallas kernels  31.4 us (23%)
  starting transfers between devices  24.4 us (18%)
  blocking collectives  22.8 us (16%)
  local copies, waits for them, and re-layouts  5.81 us (4%)
  between operations  2.28 us (2%)
  other arithmetic  2.12 us (2%)
    all_to_all x1, waiting for transfers between devices, local(): qkv = lax.all_to_all(qkv.reshape(64, 3, half, DH), 'seq', 0, 0, tiled=True)  33.8 us
    pallas_call x3, Pallas kernels, run(): pl.pallas_call(kernel, grid_spec=pltpu.PrefetchScalarGridSpec(num_scalar_...  26.7 us
    all_to_all x1, blocking collectives, local(): lax.all_to_all(mixture.reshape(64, half, DH), 'seq', 0, 0, tiled=True)  22.8 us
    ppermute x11, waiting for transfers between devices, send(): return lax.ppermute(array, AXES, pairs)  15.9 us
    all_to_all x1, starting transfers between devices, local(): qkv = lax.all_to_all(qkv.reshape(64, 3, half, DH), 'seq', 0, 0, tiled=True)  13.7 us
    ppermute x11, starting transfers between devices, send(): return lax.ppermute(array, AXES, pairs)  10.7 us
    pallas_call x1, Pallas kernels, merge(): pl.pallas_call(merge_kernel, grid_spec=pltpu.PrefetchScalarGridSpec(num_s...  4.72 us
  transfers between devices with their start and end apart: 12, of which 4 were waited for; matrix products, arithmetic and copies ran while one was open for 2% of the time, Pallas kernels for 19%

profile of v1, /device:TPU:32, one launch (start us, length us, event | category | flops | bytes accessed | tf_op | source)
XLA Modules:
  0.0 138.4 jit_solution(10819494002704100274)
XLA Ops:
  0.0 1.4 pad_maximum_fusion
  1.4 0.2 copy.11
  1.6 1.5 %copy.8 = bf16[3,2,24,2,16,128]{5,2,0,4,1,3:T(8,128)(2,1)} copy(bf16[3,2,24,2,16,128]{5,4,3,2,1,0:T(8,128)(2,1)S(1)} %bitcast.28) | data formatting | bytes 2359296 | tf_op jit(solution)/shard_map/reshape | solution.py:193
  3.1 13.7 %all-to-all-start = ((bf16[64,3,24,128]{3,2,1,0:T(8,128)(2,1)}), bf16[64,3,24,128]{3,2,1,0:T(8,128)(2,1)S(1)}, u32[]{:S(2)}, u32[]{:S(2)}) async-start(bf16[64,3,24,128]{3,2,1,0:T(8,128)(2,1)} %bitcast.4), calls=%async_computation | async-start | bytes 2359296 | tf_op jit(solution)/shard_map/all_to_all | solution.py:194
  16.8 33.8 %all-to-all-done = bf16[64,3,24,128]{3,2,1,0:T(8,128)(2,1)S(1)} async-done(((bf16[64,3,24,128]{3,2,1,0:T(8,128)(2,1)}), bf16[64,3,24,128]{3,2,1,0:T(8,128)(2,1)S(1)}, u32[]{:S(2)}, u32[]{:S(2)}) %all-to-all-start) | async-done | bytes 1179680 | tf_op jit(solution)/shard_map/all_to_all | solution.py:194
  50.6 0.2 fusion
  50.8 0.0 copy-start
  50.8 0.1 slice.26
  50.9 0.1 copy.9
  51.0 0.0 copy-start.1
  51.0 0.1 collective-permute-start
  51.1 0.0 copy-start.9
  51.1 0.1 bitcast_select_fusion
  51.2 2.2 %collective-permute-start.5 = (bf16[1536,128]{1,0:T(8,128)(2,1)S(1)}, bf16[1536,128]{1,0:T(8,128)(2,1)S(1)}, u32[]{:S(2)}, u32[]{:S(2)}) collective-permute-start(bf16[1536,128]{1,0:T(8,128)(2,1)S(1)} %bitcast_select_fusion), channel_id=1, source_target_pairs={{0,128},{1,129},{2,130},{3,131},{4,132},{5,133},{6,134},{7,135},{8... | collective-permute-start | bytes 1179656 | tf_op jit(solution)/shard_map/ppermute | solution.py:30
  53.4 1.3 collective-permute-start.6
  54.7 0.1 collective-permute-start.2
  54.8 8.6 %collective-permute-done.5.z_ref = bf16[1536,128]{1,0:T(8,128)(2,1)S(1)} collective-permute-done((bf16[1536,128]{1,0:T(8,128)(2,1)S(1)}, bf16[1536,128]{1,0:T(8,128)(2,1)S(1)}, u32[]{:S(2)}, u32[]{:S(2)}) %collective-permute-start.5) | collective-permute-done | bytes 393248 | tf_op jit(solution)/shard_map/ppermute | solution.py:30
  63.4 0.0 copy-start.4
  63.4 5.5 %collective-permute-done.6.zv_ref = bf16[1536,128]{1,0:T(8,128)(2,1)S(1)} collective-permute-done((bf16[1536,128]{1,0:T(8,128)(2,1)S(1)}, bf16[1536,128]{1,0:T(8,128)(2,1)S(1)}, u32[]{:S(2)}, u32[]{:S(2)}) %collective-permute-start.6) | collective-permute-done | bytes 393248 | tf_op jit(solution)/shard_map/ppermute | solution.py:30
  68.9 0.0 copy-start.5
  68.9 0.1 pad_maximum_fusion.1
  69.0 0.0 copy-done.1
  69.0 0.1 collective-permute-start.7
  69.1 0.0 collective-permute-done.far_ref.x_ref
  69.1 0.0 copy-start.8
  69.1 0.5 collective-permute-start.8
  69.6 0.0 copy-done
  69.6 0.1 collective-permute-start.1
  69.7 0.0 copy-done.9
  69.7 0.6 dynamic_slice.6
  72.4 1.3 dynamic_slice.7.gate_ref
  73.7 0.6 pad_add_fusion.where_ref
  74.3 0.0 collective-permute-done.1.q_core_ref
  74.3 0.0 collective-permute-done.2.core_ref
  74.3 0.0 copy-done.8
  74.3 7.1 %pair.1 = (bf16[1536,128]{1,0:T(8,128)(2,1)}, f32[8,1536]{1,0:T(8,128)}) custom-call(s32[2]{0:T(128)} %pad_add_fusion.where_ref, bf16[1536,128]{1,0:T(8,128)(2,1)} %bitcast.31, bf16[1536,128]{1,0:T(8,128)(2,1)} %collective-permute-done.1.q_core_ref, bf16[2,1536,128]{2,1,0:T(8,128)(2,1)} %copy-done.8, bf16[2,1536,128]{2,1,0:T(8,128)(2,1)} %collective-permute-done.2.core_ref), custom_call_target="tpu_custom_call" | custom-call | flops 2415919104 | tf_op jit(solution)/shard_map/pair/pallas_call | solution.py:143
  81.5 0.0 copy-done.4
  81.5 0.0 copy-done.5
  81.5 2.3 %collective-permute-start.3 = (bf16[1536,128]{1,0:T(8,128)(2,1)}, bf16[1536,128]{1,0:T(8,128)(2,1)S(1)}, u32[]{:S(2)}, u32[]{:S(2)}) collective-permute-start(bf16[1536,128]{1,0:T(8,128)(2,1)} %get-tuple-element.13.pair), channel_id=1, source_target_pairs={{0,64},{1,65},{2,66},{3,67},{4,68},{5,69},{6,70},{7,71},{8,72},{9,... | collective-permute-start | bytes 1179656 | tf_op jit(solution)/shard_map/ppermute | solution.py:30
  83.8 1.3 collective-permute-start.4
  85.1 0.0 collective-permute-done.7.zc_ref
  85.1 0.0 collective-permute-done.8.xc_ref
  85.1 10.5 %chip.1 = (bf16[1536,128]{1,0:T(8,128)(2,1)}, f32[8,1536]{1,0:T(8,128)}) custom-call(s32[2]{0:T(128)} %pad_add_fusion.where_ref, bf16[1536,128]{1,0:T(8,128)(2,1)} %bitcast.32, bf16[1536,128]{1,0:T(8,128)(2,1)} %copy-done.4, bf16[1536,128]{1,0:T(8,128)(2,1)} %copy-done.5, bf16[2,1536,128]{2,1,0:T(8,128)(2,1)} %collective-permute-done.7.zc_ref, ...), custom_call_target="tpu_custom_call" | custom-call | flops 4831838208 | tf_op jit(solution)/shard_map/chip/pallas_call | solution.py:143
  95.7 1.3 collective-permute-start.9
  97.0 1.5 %collective-permute-start.10 = (f32[8,1536]{1,0:T(8,128)}, f32[8,1536]{1,0:T(8,128)S(1)}, u32[]{:S(2)}, u32[]{:S(2)}) collective-permute-start(f32[8,1536]{1,0:T(8,128)} %get-tuple-element.16.chip_l), channel_id=1, source_target_pairs={{0,128},{1,129},{2,130},{3,131},{4,132},{5,133},{6,134},{7,135},{8... | collective-permute-start | bytes 147464 | tf_op jit(solution)/shard_map/ppermute | solution.py:30
  98.4 9.0 %own.1 = (bf16[1536,128]{1,0:T(8,128)(2,1)}, f32[8,1536]{1,0:T(8,128)}) custom-call(bf16[1536,128]{1,0:T(8,128)(2,1)} %bitcast.33, bf16[2,1536,128]{2,1,0:T(8,128)(2,1)} %bitcast.39, bf16[2,1536,128]{2,1,0:T(8,128)(2,1)} %copy-done.8), custom_call_target="tpu_custom_call" | custom-call | flops 4831838208 | tf_op jit(solution)/shard_map/own/pallas_call | solution.py:143
  107.4 0.0 collective-permute-done.4.pair_in_l
  107.4 0.0 copy-start.6
  107.4 0.0 collective-permute-done.3.pair_in
  107.5 0.0 copy-start.2
  107.5 1.7 %collective-permute-done.10.chip_in_l = f32[8,1536]{1,0:T(8,128)S(1)} collective-permute-done((f32[8,1536]{1,0:T(8,128)}, f32[8,1536]{1,0:T(8,128)S(1)}, u32[]{:S(2)}, u32[]{:S(2)}) %collective-permute-start.10) | collective-permute-done | bytes 49184 | tf_op jit(solution)/shard_map/ppermute | solution.py:30
  109.2 0.0 copy-start.7
  109.2 0.0 collective-permute-done.9.chip_in
  109.2 0.0 copy-start.3
  109.2 0.0 copy-done.6
  109.2 0.0 copy-done.2
  109.2 0.6 copy-done.7
  109.8 0.1 copy-done.3
  110.0 4.7 %merge.1 = bf16[1536,128]{1,0:T(8,128)(2,1)} custom-call(s32[2]{0:T(128)} %pad_add_fusion.where_ref, f32[1,128]{1,0:T(1,128)} %dynamic_slice.7.gate_ref, bf16[1536,128]{1,0:T(8,128)(2,1)} %get-tuple-element.11.own, f32[8,1536]{1,0:T(8,128)} %get-tuple-element.12.own_l, bf16[1536,128]{1,0:T(8,128)(2,1)} %get-tuple-element.13.pair, ...), custom_call_target="tpu_custom_call" | custom-call | tf_op jit(solution)/shard_map/merge/pallas_call | solution.py:168
  114.7 22.8 %all_to_all.10 = bf16[64,24,128]{2,1,0:T(8,128)(2,1)S(1)} all-to-all(bf16[64,24,128]{2,1,0:T(8,128)(2,1)} %bitcast.34), channel_id=1, replica_groups=mesh['stretch'=4,'seq'=64] {'seq'}, dimensions={0} | all-to-all | bytes 786432 | tf_op jit(solution)/shard_map/all_to_all | solution.py:214
  137.5 0.1 copy.13
  137.5 0.9 reshape.27
Async XLA Ops:
  3.1 47.5 %all-to-all-start = ((bf16[64,3,24,128]{3,2,1,0:T(8,128)(2,1)}), bf16[64,3,24,128]{3,2,1,0:T(8,128)(2,1)S(1)}, u32[]{:S(2)}, u32[]{:S(2)}) async-start(bf16[64,3,24,128]{3,2,1,0:T(8,128)(2,1)} %bitcast.4), calls=%async_computation | async-start | bytes 2359296 | tf_op jit(solution)/shard_map/all_to_all | solution.py:194
  50.8 18.8 %copy-start = (bf16[1,64,24,128]{3,2,0,1:T(8,128)(2,1)}, bf16[1,64,24,128]{3,2,0,1:T(8,128)(2,1)S(1)}, u32[]{:S(2)}) copy-start(bf16[1,64,24,128]{3,2,0,1:T(8,128)(2,1)S(1)} %get-tuple-element.19) | copy-start | bytes 1179652
  51.0 18.0 %copy-start.1 = (bf16[2,64,24,128]{3,2,1,0:T(8,128)(2,1)}, bf16[2,64,24,128]{3,2,1,0:T(8,128)(2,1)S(1)}, u32[]{:S(2)}) copy-start(bf16[2,64,24,128]{3,2,1,0:T(8,128)(2,1)S(1)} %copy.9) | copy-start | bytes 2359300
  51.0 18.1 %collective-permute-start = (bf16[2,1536,128]{2,1,0:T(8,128)(2,1)S(1)}, bf16[2,1536,128]{2,1,0:T(8,128)(2,1)S(1)}, u32[]{:S(2)}, u32[]{:S(2)}) collective-permute-start(bf16[2,1536,128]{2,1,0:T(8,128)(2,1)S(1)} %bitcast.37), channel_id=1, source_target_pairs={{0,16},{1,17},{2,18},{3,19},{4,20},{5,21},{6,22},{7,23},{8,24},{9,... | collective-permute-start | bytes 2359304 | tf_op jit(solution)/shard_map/ppermute | solution.py:30
  51.1 18.6 %copy-start.9 = (s32[4]{0:T(128)S(1)}, s32[4]{0:T(128)}, u32[]{:S(2)}) copy-start(s32[4]{0:T(128)} %param.8) | copy-start | bytes 52
  51.2 12.2 %collective-permute-start.5 = (bf16[1536,128]{1,0:T(8,128)(2,1)S(1)}, bf16[1536,128]{1,0:T(8,128)(2,1)S(1)}, u32[]{:S(2)}, u32[]{:S(2)}) collective-permute-start(bf16[1536,128]{1,0:T(8,128)(2,1)S(1)} %bitcast_select_fusion), channel_id=1, source_target_pairs={{0,128},{1,129},{2,130},{3,131},{4,132},{5,133},{6,134},{7,135},{8... | collective-permute-start | bytes 1179656 | tf_op jit(solution)/shard_map/ppermute | solution.py:30
  53.4 15.5 %collective-permute-start.6 = (bf16[1536,128]{1,0:T(8,128)(2,1)S(1)}, bf16[1536,128]{1,0:T(8,128)(2,1)S(1)}, u32[]{:S(2)}, u32[]{:S(2)}) collective-permute-start(bf16[1536,128]{1,0:T(8,128)(2,1)S(1)} %bitcast.40), channel_id=1, source_target_pairs={{0,128},{1,129},{2,130},{3,131},{4,132},{5,133},{6,134},{7,135},{8... | collective-permute-start | bytes 1179656 | tf_op jit(solution)/shard_map/ppermute | solution.py:30
  54.7 19.7 %collective-permute-start.2 = (bf16[2,1536,128]{2,1,0:T(8,128)(2,1)S(1)}, bf16[2,1536,128]{2,1,0:T(8,128)(2,1)}, u32[]{:S(2)}, u32[]{:S(2)}) collective-permute-start(bf16[2,1536,128]{2,1,0:T(8,128)(2,1)S(1)} %bitcast.38), channel_id=1, source_target_pairs={{0,64},{1,65},{2,66},{3,67},{4,68},{5,69},{6,70},{7,71},{8,72},{9,... | collective-permute-start | bytes 2359304 | tf_op jit(solution)/shard_map/ppermute | solution.py:30
  63.4 18.1 %copy-start.4 = (bf16[1536,128]{1,0:T(8,128)(2,1)}, bf16[1536,128]{1,0:T(8,128)(2,1)S(1)}, u32[]{:S(2)}) copy-start(bf16[1536,128]{1,0:T(8,128)(2,1)S(1)} %collective-permute-done.5.z_ref) | copy-start | bytes 1179652
  68.9 12.6 %copy-start.5 = (bf16[1536,128]{1,0:T(8,128)(2,1)}, bf16[1536,128]{1,0:T(8,128)(2,1)S(1)}, u32[]{:S(2)}) copy-start(bf16[1536,128]{1,0:T(8,128)(2,1)S(1)} %collective-permute-done.6.zv_ref) | copy-start | bytes 1179652
  69.0 16.1 %collective-permute-start.7 = (bf16[2,1536,128]{2,1,0:T(8,128)(2,1)S(1)}, bf16[2,1536,128]{2,1,0:T(8,128)(2,1)}, u32[]{:S(2)}, u32[]{:S(2)}) collective-permute-start(bf16[2,1536,128]{2,1,0:T(8,128)(2,1)S(1)} %pad_maximum_fusion.1), channel_id=1, source_target_pairs={{0,64},{1,65},{2,66},{3,67},{4,68},{5,69},{6,70},{7,71},{8,72},{9,... | collective-permute-start | bytes 2359304 | tf_op jit(solution)/shard_map/ppermute | solution.py:30
  69.1 5.2 %copy-start.8 = (bf16[2,1536,128]{2,1,0:T(8,128)(2,1)}, bf16[2,1536,128]{2,1,0:T(8,128)(2,1)S(1)}, u32[]{:S(2)}) copy-start(bf16[2,1536,128]{2,1,0:T(8,128)(2,1)S(1)} %collective-permute-done.far_ref.x_ref) | copy-start | bytes 2359300
  69.1 16.0 %collective-permute-start.8 = (bf16[2,1536,128]{2,1,0:T(8,128)(2,1)S(1)}, bf16[2,1536,128]{2,1,0:T(8,128)(2,1)}, u32[]{:S(2)}, u32[]{:S(2)}) collective-permute-start(bf16[2,1536,128]{2,1,0:T(8,128)(2,1)S(1)} %collective-permute-done.far_ref.x_ref), channel_id=1, source_target_pairs={{0,64},{1,65},{2,66},{3,67},{4,68},{5,69},{6,70},{7,71},{8,72},{9,... | collective-permute-start | bytes 2359304 | tf_op jit(solution)/shard_map/ppermute | solution.py:30
  69.6 4.7 %collective-permute-start.1 = (bf16[1536,128]{1,0:T(8,128)(2,1)S(1)}, bf16[1536,128]{1,0:T(8,128)(2,1)}, u32[]{:S(2)}, u32[]{:S(2)}) collective-permute-start(bf16[1536,128]{1,0:T(8,128)(2,1)S(1)} %bitcast.30), channel_id=1, source_target_pairs={{0,64},{1,65},{2,66},{3,67},{4,68},{5,69},{6,70},{7,71},{8,72},{9,... | collective-permute-start | bytes 1179656 | tf_op jit(solution)/shard_map/ppermute | solution.py:30
  81.5 26.0 %collective-permute-start.3 = (bf16[1536,128]{1,0:T(8,128)(2,1)}, bf16[1536,128]{1,0:T(8,128)(2,1)S(1)}, u32[]{:S(2)}, u32[]{:S(2)}) collective-permute-start(bf16[1536,128]{1,0:T(8,128)(2,1)} %get-tuple-element.13.pair), channel_id=1, source_target_pairs={{0,64},{1,65},{2,66},{3,67},{4,68},{5,69},{6,70},{7,71},{8,72},{9,... | collective-permute-start | bytes 1179656 | tf_op jit(solution)/shard_map/ppermute | solution.py:30
  83.8 23.6 %collective-permute-start.4 = (f32[8,1536]{1,0:T(8,128)}, f32[8,1536]{1,0:T(8,128)S(1)}, u32[]{:S(2)}, u32[]{:S(2)}) collective-permute-start(f32[8,1536]{1,0:T(8,128)} %get-tuple-element.14.pair_l), channel_id=1, source_target_pairs={{0,64},{1,65},{2,66},{3,67},{4,68},{5,69},{6,70},{7,71},{8,72},{9,... | collective-permute-start | bytes 147464 | tf_op jit(solution)/shard_map/ppermute | solution.py:30
  95.7 13.5 %collective-permute-start.9 = (bf16[1536,128]{1,0:T(8,128)(2,1)}, bf16[1536,128]{1,0:T(8,128)(2,1)S(1)}, u32[]{:S(2)}, u32[]{:S(2)}) collective-permute-start(bf16[1536,128]{1,0:T(8,128)(2,1)} %get-tuple-element.15.chip), channel_id=1, source_target_pairs={{0,128},{1,129},{2,130},{3,131},{4,132},{5,133},{6,134},{7,135},{8... | collective-permute-start | bytes 1179656 | tf_op jit(solution)/shard_map/ppermute | solution.py:30
  97.0 12.2 %collective-permute-start.10 = (f32[8,1536]{1,0:T(8,128)}, f32[8,1536]{1,0:T(8,128)S(1)}, u32[]{:S(2)}, u32[]{:S(2)}) collective-permute-start(f32[8,1536]{1,0:T(8,128)} %get-tuple-element.16.chip_l), channel_id=1, source_target_pairs={{0,128},{1,129},{2,130},{3,131},{4,132},{5,133},{6,134},{7,135},{8... | collective-permute-start | bytes 147464 | tf_op jit(solution)/shard_map/ppermute | solution.py:30
  107.4 1.8 %copy-start.6 = (f32[8,1536]{1,0:T(8,128)}, f32[8,1536]{1,0:T(8,128)S(1)}, u32[]{:S(2)}) copy-start(f32[8,1536]{1,0:T(8,128)S(1)} %collective-permute-done.4.pair_in_l) | copy-start | bytes 147460
  107.5 1.8 %copy-start.2 = (bf16[1536,128]{1,0:T(8,128)(2,1)}, bf16[1536,128]{1,0:T(8,128)(2,1)S(1)}, u32[]{:S(2)}) copy-start(bf16[1536,128]{1,0:T(8,128)(2,1)S(1)} %collective-permute-done.3.pair_in) | copy-start | bytes 1179652
  109.2 0.6 copy-start.7
  109.2 0.8 copy-start.3

commit v2 on v0

v2 whole, which is shorter than its diff:
```python
from functools import partial
import math

import jax
import jax.numpy as jnp
from jax import lax
from jax.experimental import pallas as pl
from jax.experimental.pallas import tpu as pltpu
from jax.sharding import PartitionSpec as P

H = 32
DH = 128
AXES = ("stretch", "seq")
SCALE = math.log2(math.e) / math.sqrt(DH)
ROWS = 512
KEYS = 512
VMEM = 24 * 2**20
F32 = jnp.float32
BF16 = jnp.bfloat16


def exchange(flip_stretch, flip_seq, keep=lambda stretch: True):
    return [
        (c * 64 + s, (c ^ flip_stretch) * 64 + (s ^ flip_seq))
        for c in range(4)
        for s in range(64)
        if keep(c)
    ]


def send(array, pairs):
    return lax.ppermute(array, AXES, pairs)


def score(q, key):
    return (
        lax.dot_general(q, key, (((1,), (1,)), ((), ())), preferred_element_type=F32) * SCALE
    )


def attend(q_ref, blocks, finish):
    work = [
        (key_ref, value_ref, at)
        for key_ref, value_ref in blocks
        for at in range(0, key_ref.shape[0], KEYS)
    ]

    def step(index, carry):
        rows = pl.ds(pl.multiple_of(index * ROWS, ROWS), ROWS)
        q = q_ref[rows, :]

        def scores_of(number):
            key_ref, _, at = work[number]
            return score(q, key_ref[at : at + KEYS, :])

        coming = scores_of(0)
        mixture = peak = None
        for number, (_, value_ref, at) in enumerate(work):
            scores = coming
            if number + 1 < len(work):
                coming = scores_of(number + 1)
            block_peak = jnp.max(scores, axis=1, keepdims=True)
            new_peak = block_peak if peak is None else jnp.maximum(peak, block_peak)
            weights = jnp.exp2(scores - new_peak).astype(BF16)
            value = value_ref[at : at + KEYS, :]
            value = jnp.concatenate([value, jnp.ones_like(value)], axis=1)
            part = jnp.dot(weights, value, preferred_element_type=F32)
            if peak is not None:
                part = mixture * jnp.exp2(peak - new_peak) + part
            mixture, peak = part, new_peak
        wide = jnp.broadcast_to(peak, (ROWS, DH))
        finish(index, rows, mixture[:, :DH], mixture[:, DH:], wide)
        return carry

    lax.fori_loop(0, q_ref.shape[0] // ROWS, step, None)


def pair(ref):
    return ref.at[0], ref.at[1]


def join(first, second):
    peak = jnp.maximum(first[2], second[2])
    left, right = jnp.exp2(first[2] - peak), jnp.exp2(second[2] - peak)
    return (
        first[0] * left + second[0] * right,
        first[1] * left + second[1] * right,
        peak,
    )


def near_kernel(q_ref, kv_ref, kvc_ref, out_ref):
    def first(index, rows, *result):
        for i in range(3):
            out_ref[i, rows, :] = result[i]

    def then(index, rows, *result):
        first(index, rows, *join(result, [out_ref[i, rows, :] for i in range(3)]))

    attend(q_ref, [pair(kv_ref)], first)

    @pl.when(lax.axis_index("stretch") % 2 == 1)
    def _():
        attend(q_ref, [pair(kvc_ref)], then)


def far_kernel(q_ref, kv_ref, kvc_ref, near_ref, chip_ref, out_ref, level_ref, state, chip_level):
    stretch = lax.axis_index("stretch")
    second = stretch % 2 == 1
    odd = stretch >= 2
    unpack_level(chip_ref, chip_level)

    def first(index, rows, *result):
        result = join(result, [near_ref[i, rows, :] for i in range(3)])
        mixture = chip_ref[rows, :].astype(F32)
        level = jnp.where(odd, chip_level[level_rows(index), :], -jnp.inf)
        level = jnp.broadcast_to(columns(level)[0], (ROWS, DH))
        result = join(result, (mixture, 1.0, level))
        for i in range(3):
            state[i, rows, :] = result[i]

    def then(index, rows, *result):
        result = join(result, [state[i, rows, :] for i in range(3)])
        for i in range(3):
            state[i, rows, :] = result[i]

    attend(q_ref, [pair(kv_ref)], first)

    @pl.when(second)
    def _():
        attend(q_ref, [pair(kvc_ref)], then)

    for index in range(q_ref.shape[0] // ROWS):
        rows = slice(index * ROWS, index * ROWS + ROWS)
        out_ref[rows, :] = state[0, rows, :] / state[1, rows, :]
        level_ref[level_rows(index), :] = level_of(state[2, rows, :], state[1, rows, :])


def level_rows(index):
    return pl.ds(index * 8 if isinstance(index, int) else pl.multiple_of(index * 8, 8), 8)


def level_of(peak, total):
    level = (peak + jnp.log2(total)).T[:1, :]
    groups = [level[:, at : at + DH] for at in range(0, ROWS, DH)]
    return jnp.concatenate((groups * 8)[:8], axis=0)


def columns(*groups):
    lines = [
        jnp.concatenate([group[at : at + 1, :] for at in range(ROWS // DH)], axis=1)
        for group in groups
    ]
    lines += [lines[0]] * (8 - len(lines))
    table = jnp.concatenate(lines, axis=0).T
    return [table[:, at : at + 1] for at in range(len(groups))]


def message_rows(span):
    return span + 3 * level_count(span)


def level_count(span):
    return -(-span // ROWS * 8 // 16) * 16


def pack_level(ref, levels):
    count = levels.shape[0]
    rest = levels[...]
    for part in range(3):
        piece = rest.astype(BF16)
        rest = rest - piece.astype(F32)
        start = ref.shape[0] - (3 - part) * count
        ref[start : start + count, :] = piece


def unpack_level(ref, levels):
    count = levels.shape[0]
    parts = [
        ref[ref.shape[0] - (3 - part) * count : ref.shape[0] - (2 - part) * count, :].astype(F32)
        for part in range(3)
    ]
    levels[...] = parts[0] + parts[1] + parts[2]


def chip_kernel(q_ref, z_ref, zc_ref, x_ref, xc_ref, out_ref, levels):
    even = lax.axis_index("stretch") < 2
    levels[...] = jnp.zeros_like(levels)

    def finish(index, rows, mixture, total, peak):
        out_ref[rows, :] = (mixture / total).astype(BF16)
        levels[level_rows(index), :] = level_of(peak, total)

    @pl.when(even)
    def _():
        attend(z_ref.at[0], [pair(x_ref), pair(xc_ref)], finish)

    @pl.when(jnp.logical_not(even))
    def _():
        attend(q_ref, [pair(z_ref), pair(zc_ref)], finish)

    pack_level(out_ref, levels)


def merge_kernel(levels_ref, gate_ref, own_ref, level_ref, chip_ref, out_ref, chip_levels):
    stretch = lax.axis_index("stretch")
    seq = lax.axis_index("seq")
    odd = stretch >= 2
    head = 16 * (seq // 32) + seq % 16
    lanes = pl.ds(pl.multiple_of(head * DH, DH), DH)
    noise = levels_ref[stretch]
    tile = gate_ref[pl.ds(pl.multiple_of(noise // 8 * 8, 8), 8), lanes]
    mine = lax.broadcasted_iota(jnp.int32, tile.shape, 0) == noise % 8
    gate = jnp.sum(jnp.where(mine, tile, 0.0), axis=0, keepdims=True)
    unpack_level(chip_ref, chip_levels)
    for index in range(own_ref.shape[0] // ROWS):
        rows = slice(index * ROWS, index * ROWS + ROWS)
        level = level_ref[level_rows(index), :]
        chip_level = jnp.where(odd, chip_levels[level_rows(index), :], -jnp.inf)
        top = jnp.maximum(level, chip_level)
        left, right = jnp.exp2(level - top), jnp.exp2(chip_level - top)
        left, right = columns(left / (left + right), right / (left + right))
        other = jnp.where(odd, chip_ref[rows, :].astype(F32), 0.0)
        attended = (own_ref[rows, :] * left + other * right).astype(BF16).astype(F32)
        out_ref[rows, :] = (gate * attended).astype(BF16)


HELD = pl.BlockSpec(memory_space=pltpu.VMEM)


def call(kernel, name, ins, in_specs, out_shape, out_spec, scratch, units):
    return pl.pallas_call(
        kernel,
        in_specs=in_specs,
        out_specs=out_spec,
        out_shape=out_shape,
        scratch_shapes=scratch,
        compiler_params=pltpu.CompilerParams(vmem_limit_bytes=VMEM),
        cost_estimate=pl.CostEstimate(
            flops=units * 8 * 1536 * 1536 * DH,
            bytes_accessed=2**20,
            transcendentals=units * 1536 * 1536,
        ),
        name=name,
    )(*ins)


def local(queries, keys, values, levels, gate_table):
    tokens = queries.shape[1]
    half = tokens // 2
    span = 64 * half
    even_chip = lax.axis_index("stretch") < 2
    qkv = jnp.concatenate([queries, keys, values])
    qkv = qkv.reshape(3, 2, half, 2, 16, DH).transpose(3, 1, 4, 0, 2, 5).reshape(64, 3, half, DH)
    qkv = lax.all_to_all(qkv, "seq", 0, 0, tiled=True)
    qkv = qkv.transpose(1, 0, 2, 3).reshape(3, span, DH)
    q, kv = qkv[0], qkv[1:]

    core, x, z = exchange(1, 0), exchange(0, 16), exchange(2, 0)
    odd_core = exchange(1, 0, lambda stretch: stretch >= 2)
    kv_x = send(kv, x)
    z = send(jnp.stack([jnp.where(even_chip, kv[0], q), kv[1]]), z)
    kv_core = send(kv, core)

    state = jax.ShapeDtypeStruct((3, span, DH), F32)
    message = jax.ShapeDtypeStruct((message_rows(span), DH), BF16)
    level_shape = (level_count(span), DH)
    level_scratch = pltpu.VMEM(level_shape, F32)
    own = [jax.ShapeDtypeStruct((span, DH), F32), jax.ShapeDtypeStruct(level_shape, F32)]
    near = call(near_kernel, "near", [q, kv, kv_core], [HELD] * 3, state, HELD, [], 2)
    kv_x, z, near = lax.optimization_barrier((kv_x, z, near))
    kv_x_core = send(kv_x, core)
    z_core = send(z, odd_core)
    chip = call(
        chip_kernel, "chip", [q, z, z_core, kv_x, kv_x_core], [HELD] * 5, message, HELD,
        [level_scratch], 2,
    )
    chip_in = send(chip, exchange(2, 0, lambda stretch: stretch < 2))
    far = call(
        far_kernel, "far", [q, kv_x, kv_x_core, near, chip], [HELD] * 5, own, [HELD] * 2,
        [pltpu.VMEM(state.shape, F32), level_scratch], 2,
    )
    mixture = call(
        merge_kernel, "merge", [levels, gate_table, *far, chip_in],
        [pl.BlockSpec(memory_space=pltpu.SMEM)] + [HELD] * 4,
        jax.ShapeDtypeStruct((span, DH), BF16), HELD, [level_scratch], 0,
    )
    result = lax.all_to_all(mixture.reshape(64, half, DH), "seq", 0, 0, tiled=True)
    result = result.reshape(2, 2, 16, half, DH).transpose(1, 3, 0, 2, 4)
    return result.reshape(1, tokens, H * DH)


def solution(mesh):
    placed = (
        P("stretch", "seq", None),
        P("stretch", "seq", None),
        P("stretch", "seq", None),
        P(),
        P(),
    )
    return jax.shard_map(
        local, mesh=mesh, in_specs=placed, out_specs=P("stretch", "seq", None), check_vma=False
    )
```

time: 438 us -> 122 us (0.28)
  the two profiles are of different devices: /device:TPU:33 before, /device:TPU:32 now
where the time goes in v2:
time: 122 us; the launch traced here: 121 us
  waiting for transfers between devices  58.5 us (48%)
  blocking collectives  22.2 us (18%)
  starting transfers between devices  20.2 us (17%)
  Pallas kernels  16 us (13%)
  local copies, waits for them, and re-layouts  2.85 us (2%)
  other arithmetic  1.51 us (1%)
    all_to_all x1, waiting for transfers between devices, local(): qkv = lax.all_to_all(qkv, 'seq', 0, 0, tiled=True)  33.8 us
    ppermute x6, waiting for transfers between devices, send(): return lax.ppermute(array, AXES, pairs)  24.8 us
    all_to_all x1, blocking collectives, local(): lax.all_to_all(mixture.reshape(64, half, DH), 'seq', 0, 0, tiled=True)  22.2 us
    pallas_call x4, Pallas kernels, call(): pl.pallas_call(kernel, in_specs=in_specs, out_specs=out_spec, out_shape=o...  16 us
    all_to_all x1, starting transfers between devices, local(): qkv = lax.all_to_all(qkv, 'seq', 0, 0, tiled=True)  13.7 us
    ppermute x6, starting transfers between devices, send(): return lax.ppermute(array, AXES, pairs)  6.52 us
  transfers between devices with their start and end apart: 7, of which 6 were waited for; matrix products, arithmetic and copies ran while one was open for 0% of the time, Pallas kernels for 7%

profile of v2, /device:TPU:32, one launch (start us, length us, event | category | flops | bytes accessed | tf_op | source)
XLA Modules:
  0.0 121.4 jit_solution(14609741069798043780)
XLA Ops:
  0.0 1.4 %pad_maximum_fusion = bf16[3,48,4096]{2,1,0:T(8,128)(2,1)S(1)} fusion(bf16[1,48,4096]{2,1,0:T(8,128)(2,1)} %param.7, bf16[1,48,4096]{2,1,0:T(8,128)(2,1)} %param.6, bf16[1,48,4096]{2,1,0:T(8,128)(2,1)} %param.5), kind=kLoop, calls=%fused_computation | loop fusion | flops 1179648 | bytes 2359296 | tf_op jit(solution)/shard_map/concatenate | solution.py:253
  1.4 0.2 copy.11
  1.6 1.5 %copy.8 = bf16[3,2,24,2,16,128]{5,2,0,4,1,3:T(8,128)(2,1)} copy(bf16[3,2,24,2,16,128]{5,4,3,2,1,0:T(8,128)(2,1)S(1)} %bitcast.28) | data formatting | bytes 2359296 | tf_op jit(solution)/shard_map/reshape | solution.py:254
  3.1 13.7 %all-to-all-start = ((bf16[64,3,24,128]{3,2,1,0:T(8,128)(2,1)}), bf16[64,3,24,128]{3,2,1,0:T(8,128)(2,1)S(1)}, u32[]{:S(2)}, u32[]{:S(2)}) async-start(bf16[64,3,24,128]{3,2,1,0:T(8,128)(2,1)} %bitcast.1), calls=%async_computation | async-start | bytes 2359296 | tf_op jit(solution)/shard_map/all_to_all | solution.py:255
  16.8 33.8 %all-to-all-done = bf16[64,3,24,128]{3,2,1,0:T(8,128)(2,1)S(1)} async-done(((bf16[64,3,24,128]{3,2,1,0:T(8,128)(2,1)}), bf16[64,3,24,128]{3,2,1,0:T(8,128)(2,1)S(1)}, u32[]{:S(2)}, u32[]{:S(2)}) %all-to-all-start) | async-done | bytes 1179680 | tf_op jit(solution)/shard_map/all_to_all | solution.py:255
  50.5 0.1 slice.29
  50.6 0.1 copy.9
  50.7 0.1 collective-permute-start.2
  50.8 0.1 collective-permute-start
  51.0 0.1 slice_select_fusion
  51.0 0.1 pad_maximum_fusion.1
  51.1 2.2 %collective-permute-start.1 = (bf16[2,1536,128]{2,1,0:T(8,128)(2,1)S(1)}, bf16[2,1536,128]{2,1,0:T(8,128)(2,1)S(1)}, u32[]{:S(2)}, u32[]{:S(2)}) collective-permute-start(bf16[2,1536,128]{2,1,0:T(8,128)(2,1)S(1)} %pad_maximum_fusion.1), channel_id=1, source_target_pairs={{0,128},{1,129},{2,130},{3,131},{4,132},{5,133},{6,134},{7,135},{8... | collective-permute-start | bytes 2359304 | tf_op jit(solution)/shard_map/ppermute | solution.py:32
  53.3 0.0 collective-permute-done.2.kvc_ref
  53.3 3.6 %near.1.near_ref = f32[3,1536,128]{2,1,0:T(8,128)S(1)} custom-call(bf16[1536,128]{1,0:T(8,128)(2,1)S(1)} %bitcast.23, bf16[2,1536,128]{2,1,0:T(8,128)(2,1)S(1)} %bitcast.22, bf16[2,1536,128]{2,1,0:T(8,128)(2,1)S(1)} %collective-permute-done.2.kvc_ref), custom_call_target="tpu_custom_call" | custom-call | flops 4831838208 | bytes 1048576 | tf_op jit(solution)/shard_map/near/pallas_call | solution.py:232
  56.9 13.9 %collective-permute-done.x_ref.kv_ref = bf16[2,1536,128]{2,1,0:T(8,128)(2,1)S(1)} collective-permute-done((bf16[2,1536,128]{2,1,0:T(8,128)(2,1)S(1)}, bf16[2,1536,128]{2,1,0:T(8,128)(2,1)S(1)}, u32[]{:S(2)}, u32[]{:S(2)}) %collective-permute-start) | collective-permute-done | bytes 786464 | tf_op jit(solution)/shard_map/ppermute | solution.py:32
  70.8 0.6 collective-permute-done.1.z_ref
  71.4 1.9 %collective-permute-start.4 = (bf16[2,1536,128]{2,1,0:T(8,128)(2,1)S(1)}, bf16[2,1536,128]{2,1,0:T(8,128)(2,1)S(1)}, u32[]{:S(2)}, u32[]{:S(2)}) collective-permute-start(bf16[2,1536,128]{2,1,0:T(8,128)(2,1)S(1)} %collective-permute-done.1.z_ref), channel_id=1, source_target_pairs={{128,192},{129,193},{130,194},{131,195},{132,196},{133,197},{134,1... | collective-permute-start | bytes 2359304 | tf_op jit(solution)/shard_map/ppermute | solution.py:32
  73.3 0.6 collective-permute-start.3
  73.9 1.7 %collective-permute-done.4.zc_ref = bf16[2,1536,128]{2,1,0:T(8,128)(2,1)S(1)} collective-permute-done((bf16[2,1536,128]{2,1,0:T(8,128)(2,1)S(1)}, bf16[2,1536,128]{2,1,0:T(8,128)(2,1)S(1)}, u32[]{:S(2)}, u32[]{:S(2)}) %collective-permute-start.4) | collective-permute-done | bytes 786464 | tf_op jit(solution)/shard_map/ppermute | solution.py:32
  75.5 1.1 collective-permute-done.3.xc_ref.kvc_ref
  76.7 6.5 %chip.1.chip_ref = bf16[1632,128]{1,0:T(8,128)(2,1)S(1)} custom-call(bf16[1536,128]{1,0:T(8,128)(2,1)S(1)} %bitcast.24, bf16[2,1536,128]{2,1,0:T(8,128)(2,1)S(1)} %collective-permute-done.1.z_ref, bf16[2,1536,128]{2,1,0:T(8,128)(2,1)S(1)} %collective-permute-done.4.zc_ref, bf16[2,1536,128]{2,1,0:T(8,128)(2,1)S(1)} %collective-permute-done.x_ref.kv_ref, ...), custom_call_target="tpu_custom_call" | custom-call | flops 4831838208 | bytes 1048576 | tf_op jit(solution)/shard_map/chip/pallas_call | solution.py:232
  83.2 0.0 copy-start
  83.2 0.0 copy-start.1
  83.2 1.6 %collective-permute-start.5 = (bf16[1632,128]{1,0:T(8,128)(2,1)S(1)}, bf16[1632,128]{1,0:T(8,128)(2,1)S(1)}, u32[]{:S(2)}, u32[]{:S(2)}) collective-permute-start(bf16[1632,128]{1,0:T(8,128)(2,1)S(1)} %chip.1.chip_ref), channel_id=1, source_target_pairs={{0,128},{1,129},{2,130},{3,131},{4,132},{5,133},{6,134},{7,135},{8... | collective-permute-start | bytes 1253384 | tf_op jit(solution)/shard_map/ppermute | solution.py:32
  84.8 4.6 %far.1 = (f32[1536,128]{1,0:T(8,128)S(1)}, f32[32,128]{1,0:T(8,128)S(1)}) custom-call(bf16[1536,128]{1,0:T(8,128)(2,1)S(1)} %bitcast.25, bf16[2,1536,128]{2,1,0:T(8,128)(2,1)S(1)} %collective-permute-done.x_ref.kv_ref, bf16[2,1536,128]{2,1,0:T(8,128)(2,1)S(1)} %collective-permute-done.3.xc_ref.kvc_ref, f32[3,1536,128]{2,1,0:T(8,128)S(1)} %near.1.near_ref, ...), custom_call_target="tpu_custom_call" | custom-call | flops 4831838208 | bytes 1048576 | tf_op jit(solution)/shard_map/far/pallas_call | solution.py:232
  89.4 7.5 %collective-permute-done.5.chip_ref = bf16[1632,128]{1,0:T(8,128)(2,1)S(1)} collective-permute-done((bf16[1632,128]{1,0:T(8,128)(2,1)S(1)}, bf16[1632,128]{1,0:T(8,128)(2,1)S(1)}, u32[]{:S(2)}, u32[]{:S(2)}) %collective-permute-start.5) | collective-permute-done | bytes 417824 | tf_op jit(solution)/shard_map/ppermute | solution.py:32
  96.9 0.0 copy-done
  96.9 0.0 copy-done.1
  96.9 1.3 %merge.1 = bf16[1536,128]{1,0:T(8,128)(2,1)S(1)} custom-call(s32[4]{0:T(128)S(1)} %copy-done.1, f32[64,4096]{1,0:T(8,128)S(1)} %copy-done, f32[1536,128]{1,0:T(8,128)S(1)} %get-tuple-element.13.own_ref, f32[32,128]{1,0:T(8,128)S(1)} %get-tuple-element.14.level_ref, bf16[1632,128]{1,0:T(8,128)(2,1)S(1)} %collective-permute-done.5.chip_ref), custom_call_target="tpu_custom_call" | custom-call | bytes 1048576 | tf_op jit(solution)/shard_map/merge/pallas_call | solution.py:232
  98.2 22.2 %all_to_all.10 = bf16[64,24,128]{2,1,0:T(8,128)(2,1)S(1)} all-to-all(bf16[64,24,128]{2,1,0:T(8,128)(2,1)S(1)} %bitcast.19), channel_id=1, replica_groups=mesh['stretch'=4,'seq'=64] {'seq'}, dimensions={0} | all-to-all | bytes 786432 | tf_op jit(solution)/shard_map/all_to_all | solution.py:288
  120.5 0.1 copy.13
  120.5 0.9 reshape.45
Async XLA Ops:
  3.1 47.5 %all-to-all-start = ((bf16[64,3,24,128]{3,2,1,0:T(8,128)(2,1)}), bf16[64,3,24,128]{3,2,1,0:T(8,128)(2,1)S(1)}, u32[]{:S(2)}, u32[]{:S(2)}) async-start(bf16[64,3,24,128]{3,2,1,0:T(8,128)(2,1)} %bitcast.1), calls=%async_computation | async-start | bytes 2359296 | tf_op jit(solution)/shard_map/all_to_all | solution.py:255
  50.7 2.6 %collective-permute-start.2 = (bf16[2,1536,128]{2,1,0:T(8,128)(2,1)S(1)}, bf16[2,1536,128]{2,1,0:T(8,128)(2,1)S(1)}, u32[]{:S(2)}, u32[]{:S(2)}) collective-permute-start(bf16[2,1536,128]{2,1,0:T(8,128)(2,1)S(1)} %bitcast.20), channel_id=1, source_target_pairs={{0,64},{1,65},{2,66},{3,67},{4,68},{5,69},{6,70},{7,71},{8,72},{9,... | collective-permute-start | bytes 2359304 | tf_op jit(solution)/shard_map/ppermute | solution.py:32
  50.8 20.0 %collective-permute-start = (bf16[2,1536,128]{2,1,0:T(8,128)(2,1)S(1)}, bf16[2,1536,128]{2,1,0:T(8,128)(2,1)S(1)}, u32[]{:S(2)}, u32[]{:S(2)}) collective-permute-start(bf16[2,1536,128]{2,1,0:T(8,128)(2,1)S(1)} %bitcast.21), channel_id=1, source_target_pairs={{0,16},{1,17},{2,18},{3,19},{4,20},{5,21},{6,22},{7,23},{8,24},{9,... | collective-permute-start | bytes 2359304 | tf_op jit(solution)/shard_map/ppermute | solution.py:32
  51.1 20.3 %collective-permute-start.1 = (bf16[2,1536,128]{2,1,0:T(8,128)(2,1)S(1)}, bf16[2,1536,128]{2,1,0:T(8,128)(2,1)S(1)}, u32[]{:S(2)}, u32[]{:S(2)}) collective-permute-start(bf16[2,1536,128]{2,1,0:T(8,128)(2,1)S(1)} %pad_maximum_fusion.1), channel_id=1, source_target_pairs={{0,128},{1,129},{2,130},{3,131},{4,132},{5,133},{6,134},{7,135},{8... | collective-permute-start | bytes 2359304 | tf_op jit(solution)/shard_map/ppermute | solution.py:32
  71.4 4.2 %collective-permute-start.4 = (bf16[2,1536,128]{2,1,0:T(8,128)(2,1)S(1)}, bf16[2,1536,128]{2,1,0:T(8,128)(2,1)S(1)}, u32[]{:S(2)}, u32[]{:S(2)}) collective-permute-start(bf16[2,1536,128]{2,1,0:T(8,128)(2,1)S(1)} %collective-permute-done.1.z_ref), channel_id=1, source_target_pairs={{128,192},{129,193},{130,194},{131,195},{132,196},{133,197},{134,1... | collective-permute-start | bytes 2359304 | tf_op jit(solution)/shard_map/ppermute | solution.py:32
  73.3 3.4 %collective-permute-start.3 = (bf16[2,1536,128]{2,1,0:T(8,128)(2,1)S(1)}, bf16[2,1536,128]{2,1,0:T(8,128)(2,1)S(1)}, u32[]{:S(2)}, u32[]{:S(2)}) collective-permute-start(bf16[2,1536,128]{2,1,0:T(8,128)(2,1)S(1)} %collective-permute-done.x_ref.kv_ref), channel_id=1, source_target_pairs={{0,64},{1,65},{2,66},{3,67},{4,68},{5,69},{6,70},{7,71},{8,72},{9,... | collective-permute-start | bytes 2359304 | tf_op jit(solution)/shard_map/ppermute | solution.py:32
  83.2 13.7 %copy-start = (f32[64,4096]{1,0:T(8,128)S(1)}, f32[64,4096]{1,0:T(8,128)}, u32[]{:S(2)}) copy-start(f32[64,4096]{1,0:T(8,128)} %gate_ref.1) | copy-start | bytes 3145732
  83.2 13.7 %copy-start.1 = (s32[4]{0:T(128)S(1)}, s32[4]{0:T(128)}, u32[]{:S(2)}) copy-start(s32[4]{0:T(128)} %levels_ref.1) | copy-start | bytes 52
  83.2 13.7 %collective-permute-start.5 = (bf16[1632,128]{1,0:T(8,128)(2,1)S(1)}, bf16[1632,128]{1,0:T(8,128)(2,1)S(1)}, u32[]{:S(2)}, u32[]{:S(2)}) collective-permute-start(bf16[1632,128]{1,0:T(8,128)(2,1)S(1)} %chip.1.chip_ref), channel_id=1, source_target_pairs={{0,128},{1,129},{2,130},{3,131},{4,132},{5,133},{6,134},{7,135},{8... | collective-permute-start | bytes 1253384 | tf_op jit(solution)/shard_map/ppermute | solution.py:32

commit v3 on v2

--- a/solution.py
+++ b/solution.py
@@ -104,18 +104,11 @@
         attend(q_ref, [pair(kvc_ref)], then)
 
 
-def far_kernel(q_ref, kv_ref, kvc_ref, near_ref, chip_ref, out_ref, level_ref, state, chip_level):
-    stretch = lax.axis_index("stretch")
-    second = stretch % 2 == 1
-    odd = stretch >= 2
-    unpack_level(chip_ref, chip_level)
+def far_kernel(q_ref, kv_ref, kvc_ref, near_ref, out_ref, level_ref, state):
+    second = lax.axis_index("stretch") % 2 == 1
 
     def first(index, rows, *result):
         result = join(result, [near_ref[i, rows, :] for i in range(3)])
-        mixture = chip_ref[rows, :].astype(F32)
-        level = jnp.where(odd, chip_level[level_rows(index), :], -jnp.inf)
-        level = jnp.broadcast_to(columns(level)[0], (ROWS, DH))
-        result = join(result, (mixture, 1.0, level))
         for i in range(3):
             state[i, rows, :] = result[i]
 
@@ -183,23 +176,27 @@
     levels[...] = parts[0] + parts[1] + parts[2]
 
 
-def chip_kernel(q_ref, z_ref, zc_ref, x_ref, xc_ref, out_ref, levels):
-    even = lax.axis_index("stretch") < 2
-    levels[...] = jnp.zeros_like(levels)
-
-    def finish(index, rows, mixture, total, peak):
+def chip_near_kernel(q_ref, kv_ref, kvc_ref, out_ref):
+    def finish(index, rows, *result):
+        for i in range(3):
+            out_ref[i, rows, :] = result[i]
+
+    @pl.when(lax.axis_index("stretch") < 2)
+    def _():
+        attend(q_ref, [pair(kv_ref), pair(kvc_ref)], finish)
+
+
+def chip_far_kernel(q_ref, kv_ref, kvc_ref, near_ref, out_ref, levels):
+    def finish(index, rows, *result):
+        mixture, total, peak = join(result, [near_ref[i, rows, :] for i in range(3)])
         out_ref[rows, :] = (mixture / total).astype(BF16)
         levels[level_rows(index), :] = level_of(peak, total)
 
-    @pl.when(even)
+    @pl.when(lax.axis_index("stretch") < 2)
     def _():
-        attend(z_ref.at[0], [pair(x_ref), pair(xc_ref)], finish)
-
-    @pl.when(jnp.logical_not(even))
-    def _():
-        attend(q_ref, [pair(z_ref), pair(zc_ref)], finish)
-
-    pack_level(out_ref, levels)
+        levels[...] = jnp.zeros_like(levels)
+        attend(q_ref, [pair(kv_ref), pair(kvc_ref)], finish)
+        pack_level(out_ref, levels)
 
 
 def merge_kernel(levels_ref, gate_ref, own_ref, level_ref, chip_ref, out_ref, chip_levels):
@@ -249,36 +246,37 @@
     tokens = queries.shape[1]
     half = tokens // 2
     span = 64 * half
-    even_chip = lax.axis_index("stretch") < 2
     qkv = jnp.concatenate([queries, keys, values])
     qkv = qkv.reshape(3, 2, half, 2, 16, DH).transpose(3, 1, 4, 0, 2, 5).reshape(64, 3, half, DH)
     qkv = lax.all_to_all(qkv, "seq", 0, 0, tiled=True)
     qkv = qkv.transpose(1, 0, 2, 3).reshape(3, span, DH)
     q, kv = qkv[0], qkv[1:]
 
-    core, x, z = exchange(1, 0), exchange(0, 16), exchange(2, 0)
-    odd_core = exchange(1, 0, lambda stretch: stretch >= 2)
-    kv_x = send(kv, x)
-    z = send(jnp.stack([jnp.where(even_chip, kv[0], q), kv[1]]), z)
+    core = exchange(1, 0)
+    kv_x = send(kv, exchange(0, 16))
     kv_core = send(kv, core)
-
+    q_z = send(q, exchange(2, 0, lambda stretch: stretch >= 2))
     state = jax.ShapeDtypeStruct((3, span, DH), F32)
     message = jax.ShapeDtypeStruct((message_rows(span), DH), BF16)
     level_shape = (level_count(span), DH)
     level_scratch = pltpu.VMEM(level_shape, F32)
     own = [jax.ShapeDtypeStruct((span, DH), F32), jax.ShapeDtypeStruct(level_shape, F32)]
     near = call(near_kernel, "near", [q, kv, kv_core], [HELD] * 3, state, HELD, [], 2)
-    kv_x, z, near = lax.optimization_barrier((kv_x, z, near))
+    q_z, near = lax.optimization_barrier((q_z, near))
+    chip_near = call(
+        chip_near_kernel, "chip_near", [q_z, kv, kv_core], [HELD] * 3, state, HELD, [], 2
+    )
+    kv_x, near, chip_near = lax.optimization_barrier((kv_x, near, chip_near))
     kv_x_core = send(kv_x, core)
-    z_core = send(z, odd_core)
     chip = call(
-        chip_kernel, "chip", [q, z, z_core, kv_x, kv_x_core], [HELD] * 5, message, HELD,
+        chip_far_kernel, "chip_far", [q_z, kv_x, kv_x_core, chip_near], [HELD] * 4, message, HELD,
         [level_scratch], 2,
     )
     chip_in = send(chip, exchange(2, 0, lambda stretch: stretch < 2))
+    chip, near = lax.optimization_barrier((chip, near))
     far = call(
-        far_kernel, "far", [q, kv_x, kv_x_core, near, chip], [HELD] * 5, own, [HELD] * 2,
-        [pltpu.VMEM(state.shape, F32), level_scratch], 2,
+        far_kernel, "far", [q, kv_x, kv_x_core, near], [HELD] * 4, own, [HELD] * 2,
+        [pltpu.VMEM(state.shape, F32)], 2,
     )
     mixture = call(
         merge_kernel, "merge", [levels, gate_table, *far, chip_in],

time: 122 us -> 117 us (0.959)
  blocking collectives: 22.2 us -> 69.1 us
  waiting for transfers between devices: 58.5 us -> 29.3 us
  starting transfers between devices: 20.2 us -> 5.82 us
  Pallas kernels: 16 us -> 9 us
    all_to_all x0 -> x1, blocking collectives: none -> 47.2 us  [local(): qkv = lax.all_to_all(qkv, 'seq', 0, 0, tiled=True)]
    all_to_all x1 -> x0, waiting for transfers between devices: 33.8 us -> none  [local(): qkv = lax.all_to_all(qkv, 'seq', 0, 0, tiled=True)]
    all_to_all x1 -> x0, starting transfers between devices: 13.7 us -> none  [local(): qkv = lax.all_to_all(qkv, 'seq', 0, 0, tiled=True)]
    pallas_call x4 -> x5, Pallas kernels: 16 us -> 9 us  [call(): pl.pallas_call(kernel, in_specs=in_specs, out_specs=out_spec, out_shape=o...]
    ppermute x6 -> x5, waiting for transfers between devices: 24.8 us -> 29.3 us  [send(): return lax.ppermute(array, AXES, pairs)]
    ppermute x6 -> x5, starting transfers between devices: 6.52 us -> 5.82 us  [send(): return lax.ppermute(array, AXES, pairs)]
  transfers between devices with their start and end apart: 7 -> 5, of which waited for: 6 -> 4; matrix products, arithmetic and copies ran while one was open for 0% -> 0% of each run, Pallas kernels for 7% -> 7%
where the time goes in v3:
time: 117 us
  blocking collectives  69.1 us (59%)
  waiting for transfers between devices  29.3 us (25%)
  Pallas kernels  9 us (8%)
  starting transfers between devices  5.82 us (5%)
  local copies, waits for them, and re-layouts  1.87 us (2%)
  other arithmetic  1.36 us (1%)
    all_to_all x1, blocking collectives, local(): qkv = lax.all_to_all(qkv, 'seq', 0, 0, tiled=True)  47.2 us
    ppermute x5, waiting for transfers between devices, send(): return lax.ppermute(array, AXES, pairs)  29.3 us
    all_to_all x1, blocking collectives, local(): lax.all_to_all(mixture.reshape(64, half, DH), 'seq', 0, 0, tiled=True)  21.8 us
    pallas_call x5, Pallas kernels, call(): pl.pallas_call(kernel, in_specs=in_specs, out_specs=out_spec, out_shape=o...  9 us
    ppermute x5, starting transfers between devices, send(): return lax.ppermute(array, AXES, pairs)  5.82 us
  transfers between devices with their start and end apart: 5, of which 4 were waited for; matrix products, arithmetic and copies ran while one was open for 0% of the time, Pallas kernels for 7%

profile of v3, /device:TPU:32, one launch (start us, length us, event | category | flops | bytes accessed | tf_op | source)
XLA Modules:
  0.0 116.5 jit_solution(14683573091540351346)
XLA Ops:
  0.0 1.4 %pad_maximum_fusion = bf16[3,48,4096]{2,1,0:T(8,128)(2,1)S(1)} fusion(bf16[1,48,4096]{2,1,0:T(8,128)(2,1)} %param.7, bf16[1,48,4096]{2,1,0:T(8,128)(2,1)} %param.6, bf16[1,48,4096]{2,1,0:T(8,128)(2,1)} %param.5), kind=kLoop, calls=%fused_computation | loop fusion | flops 1179648 | bytes 2359296 | tf_op jit(solution)/shard_map/concatenate | solution.py:249
  1.4 0.2 copy.11
  1.6 0.5 copy.8
  2.1 47.2 %all_to_all.10 = bf16[64,3,24,128]{3,2,1,0:T(8,128)(2,1)S(1)} all-to-all(bf16[64,3,24,128]{3,2,1,0:T(8,128)(2,1)S(1)} %bitcast.28), channel_id=1, replica_groups=mesh['stretch'=4,'seq'=64] {'seq'}, dimensions={0} | all-to-all | bytes 2359296 | tf_op jit(solution)/shard_map/all_to_all | solution.py:251
  49.3 0.1 slice.14
  49.4 0.1 copy.9
  49.5 0.1 collective-permute-start.2
  49.6 0.1 collective-permute-start
  49.8 4.0 %collective-permute-start.1 = (bf16[1536,128]{1,0:T(8,128)(2,1)S(1)}, bf16[1536,128]{1,0:T(8,128)(2,1)S(1)}, u32[]{:S(2)}, u32[]{:S(2)}) collective-permute-start(bf16[1536,128]{1,0:T(8,128)(2,1)S(1)} %bitcast.22), channel_id=1, source_target_pairs={{128,0},{129,1},{130,2},{131,3},{132,4},{133,5},{134,6},{135,7},{1... | collective-permute-start | bytes 1179656 | tf_op jit(solution)/shard_map/ppermute | solution.py:32
  53.8 0.0 collective-permute-done.2.kvc_ref
  53.8 3.6 %near.1.near_ref = f32[3,1536,128]{2,1,0:T(8,128)S(1)} custom-call(bf16[1536,128]{1,0:T(8,128)(2,1)S(1)} %bitcast.23, bf16[2,1536,128]{2,1,0:T(8,128)(2,1)S(1)} %bitcast.20, bf16[2,1536,128]{2,1,0:T(8,128)(2,1)S(1)} %collective-permute-done.2.kvc_ref), custom_call_target="tpu_custom_call" | custom-call | flops 4831838208 | bytes 1048576 | tf_op jit(solution)/shard_map/near/pallas_call | solution.py:229
  57.4 5.4 %collective-permute-done.1.q_ref = bf16[1536,128]{1,0:T(8,128)(2,1)S(1)} collective-permute-done((bf16[1536,128]{1,0:T(8,128)(2,1)S(1)}, bf16[1536,128]{1,0:T(8,128)(2,1)S(1)}, u32[]{:S(2)}, u32[]{:S(2)}) %collective-permute-start.1) | collective-permute-done | bytes 393248 | tf_op jit(solution)/shard_map/ppermute | solution.py:32
  62.8 6.9 %collective-permute-done.kv_ref = bf16[2,1536,128]{2,1,0:T(8,128)(2,1)S(1)} collective-permute-done((bf16[2,1536,128]{2,1,0:T(8,128)(2,1)S(1)}, bf16[2,1536,128]{2,1,0:T(8,128)(2,1)S(1)}, u32[]{:S(2)}, u32[]{:S(2)}) %collective-permute-start) | collective-permute-done | bytes 786464 | tf_op jit(solution)/shard_map/ppermute | solution.py:32
  69.7 0.0 collective-permute-start.3
  69.7 2.3 %collective-permute-done.3.kvc_ref = bf16[2,1536,128]{2,1,0:T(8,128)(2,1)S(1)} collective-permute-done((bf16[2,1536,128]{2,1,0:T(8,128)(2,1)S(1)}, bf16[2,1536,128]{2,1,0:T(8,128)(2,1)S(1)}, u32[]{:S(2)}, u32[]{:S(2)}) %collective-permute-start.3) | collective-permute-done | bytes 786464 | tf_op jit(solution)/shard_map/ppermute | solution.py:32
  72.0 0.0 copy-start
  72.0 0.0 copy-start.1
  72.0 1.6 %collective-permute-start.4 = (bf16[1632,128]{1,0:T(8,128)(2,1)S(1)}, bf16[1632,128]{1,0:T(8,128)(2,1)S(1)}, u32[]{:S(2)}, u32[]{:S(2)}) collective-permute-start(bf16[1632,128]{1,0:T(8,128)(2,1)S(1)} %chip_far.1), channel_id=1, source_target_pairs={{0,128},{1,129},{2,130},{3,131},{4,132},{5,133},{6,134},{7,135},{8... | collective-permute-start | bytes 1253384 | tf_op jit(solution)/shard_map/ppermute | solution.py:32
  73.6 4.1 %far.1 = (f32[1536,128]{1,0:T(8,128)S(1)}, f32[32,128]{1,0:T(8,128)S(1)}) custom-call(bf16[1536,128]{1,0:T(8,128)(2,1)S(1)} %bitcast.24, bf16[2,1536,128]{2,1,0:T(8,128)(2,1)S(1)} %collective-permute-done.kv_ref, bf16[2,1536,128]{2,1,0:T(8,128)(2,1)S(1)} %collective-permute-done.3.kvc_ref, f32[3,1536,128]{2,1,0:T(8,128)S(1)} %near.1.near_ref), custom_call_target="tpu_custom_call" | custom-call | flops 4831838208 | bytes 1048576 | tf_op jit(solution)/shard_map/far/pallas_call | solution.py:229
  77.7 14.7 %collective-permute-done.4.chip_ref = bf16[1632,128]{1,0:T(8,128)(2,1)S(1)} collective-permute-done((bf16[1632,128]{1,0:T(8,128)(2,1)S(1)}, bf16[1632,128]{1,0:T(8,128)(2,1)S(1)}, u32[]{:S(2)}, u32[]{:S(2)}) %collective-permute-start.4) | collective-permute-done | bytes 417824 | tf_op jit(solution)/shard_map/ppermute | solution.py:32
  92.4 0.0 copy-done
  92.4 0.0 copy-done.1
  92.4 1.3 %merge.1 = bf16[1536,128]{1,0:T(8,128)(2,1)S(1)} custom-call(s32[4]{0:T(128)S(1)} %copy-done.1, f32[64,4096]{1,0:T(8,128)S(1)} %copy-done, f32[1536,128]{1,0:T(8,128)S(1)} %get-tuple-element.19.own_ref, f32[32,128]{1,0:T(8,128)S(1)} %get-tuple-element.20.level_ref, bf16[1632,128]{1,0:T(8,128)(2,1)S(1)} %collective-permute-done.4.chip_ref), custom_call_target="tpu_custom_call" | custom-call | bytes 1048576 | tf_op jit(solution)/shard_map/merge/pallas_call | solution.py:229
  93.7 21.8 %all_to_all.11 = bf16[64,24,128]{2,1,0:T(8,128)(2,1)S(1)} all-to-all(bf16[64,24,128]{2,1,0:T(8,128)(2,1)S(1)} %bitcast.17), channel_id=1, replica_groups=mesh['stretch'=4,'seq'=64] {'seq'}, dimensions={0} | all-to-all | bytes 786432 | tf_op jit(solution)/shard_map/all_to_all | solution.py:286
  115.6 0.1 copy.13
  115.6 0.9 reshape.23
  (3 shorter events, 0.0 us)
Async XLA Ops:
  49.5 4.3 %collective-permute-start.2 = (bf16[2,1536,128]{2,1,0:T(8,128)(2,1)S(1)}, bf16[2,1536,128]{2,1,0:T(8,128)(2,1)S(1)}, u32[]{:S(2)}, u32[]{:S(2)}) collective-permute-start(bf16[2,1536,128]{2,1,0:T(8,128)(2,1)S(1)} %bitcast.18), channel_id=1, source_target_pairs={{0,64},{1,65},{2,66},{3,67},{4,68},{5,69},{6,70},{7,71},{8,72},{9,... | collective-permute-start | bytes 2359304 | tf_op jit(solution)/shard_map/ppermute | solution.py:32
  49.6 20.0 %collective-permute-start = (bf16[2,1536,128]{2,1,0:T(8,128)(2,1)S(1)}, bf16[2,1536,128]{2,1,0:T(8,128)(2,1)S(1)}, u32[]{:S(2)}, u32[]{:S(2)}) collective-permute-start(bf16[2,1536,128]{2,1,0:T(8,128)(2,1)S(1)} %bitcast.19), channel_id=1, source_target_pairs={{0,16},{1,17},{2,18},{3,19},{4,20},{5,21},{6,22},{7,23},{8,24},{9,... | collective-permute-start | bytes 2359304 | tf_op jit(solution)/shard_map/ppermute | solution.py:32
  49.8 13.0 %collective-permute-start.1 = (bf16[1536,128]{1,0:T(8,128)(2,1)S(1)}, bf16[1536,128]{1,0:T(8,128)(2,1)S(1)}, u32[]{:S(2)}, u32[]{:S(2)}) collective-permute-start(bf16[1536,128]{1,0:T(8,128)(2,1)S(1)} %bitcast.22), channel_id=1, source_target_pairs={{128,0},{129,1},{130,2},{131,3},{132,4},{133,5},{134,6},{135,7},{1... | collective-permute-start | bytes 1179656 | tf_op jit(solution)/shard_map/ppermute | solution.py:32
  69.7 2.3 %collective-permute-start.3 = (bf16[2,1536,128]{2,1,0:T(8,128)(2,1)S(1)}, bf16[2,1536,128]{2,1,0:T(8,128)(2,1)S(1)}, u32[]{:S(2)}, u32[]{:S(2)}) collective-permute-start(bf16[2,1536,128]{2,1,0:T(8,128)(2,1)S(1)} %collective-permute-done.kv_ref), channel_id=1, source_target_pairs={{0,64},{1,65},{2,66},{3,67},{4,68},{5,69},{6,70},{7,71},{8,72},{9,... | collective-permute-start | bytes 2359304 | tf_op jit(solution)/shard_map/ppermute | solution.py:32
  72.0 20.5 %copy-start = (f32[64,4096]{1,0:T(8,128)S(1)}, f32[64,4096]{1,0:T(8,128)}, u32[]{:S(2)}) copy-start(f32[64,4096]{1,0:T(8,128)} %gate_ref.1) | copy-start | bytes 3145732
  72.0 20.5 %copy-start.1 = (s32[4]{0:T(128)S(1)}, s32[4]{0:T(128)}, u32[]{:S(2)}) copy-start(s32[4]{0:T(128)} %levels_ref.1) | copy-start | bytes 52
  72.0 20.5 %collective-permute-start.4 = (bf16[1632,128]{1,0:T(8,128)(2,1)S(1)}, bf16[1632,128]{1,0:T(8,128)(2,1)S(1)}, u32[]{:S(2)}, u32[]{:S(2)}) collective-permute-start(bf16[1632,128]{1,0:T(8,128)(2,1)S(1)} %chip_far.1), channel_id=1, source_target_pairs={{0,128},{1,129},{2,130},{3,131},{4,132},{5,133},{6,134},{7,135},{8... | collective-permute-start | bytes 1253384 | tf_op jit(solution)/shard_map/ppermute | solution.py:32

commit v4 on v3

--- a/solution.py
+++ b/solution.py
@@ -12,7 +12,7 @@
 DH = 128
 AXES = ("stretch", "seq")
 SCALE = math.log2(math.e) / math.sqrt(DH)
-ROWS = 512
+ROWS = 768
 KEYS = 512
 VMEM = 24 * 2**20
 F32 = jnp.float32
@@ -38,7 +38,7 @@
     )
 
 
-def attend(q_ref, blocks, finish):
+def attend(q_ref, blocks, finish, first=0, count=None):
     work = [
         (key_ref, value_ref, at)
         for key_ref, value_ref in blocks
@@ -72,7 +72,8 @@
         finish(index, rows, mixture[:, :DH], mixture[:, DH:], wide)
         return carry
 
-    lax.fori_loop(0, q_ref.shape[0] // ROWS, step, None)
+    count = q_ref.shape[0] // ROWS if count is None else count
+    lax.fori_loop(first, first + count, step, None)
 
 
 def pair(ref):
@@ -89,44 +90,54 @@
     )
 
 
+def by_core(q_ref, blocks, core_block, finish):
+    second = lax.axis_index("stretch") % 2 == 1
+    pl.when(second)(lambda: attend(q_ref, [*blocks, core_block], finish))
+    pl.when(jnp.logical_not(second))(lambda: attend(q_ref, blocks, finish))
+
+
 def near_kernel(q_ref, kv_ref, kvc_ref, out_ref):
-    def first(index, rows, *result):
+    def finish(index, rows, *result):
         for i in range(3):
             out_ref[i, rows, :] = result[i]
 
-    def then(index, rows, *result):
-        first(index, rows, *join(result, [out_ref[i, rows, :] for i in range(3)]))
-
-    attend(q_ref, [pair(kv_ref)], first)
-
-    @pl.when(lax.axis_index("stretch") % 2 == 1)
-    def _():
-        attend(q_ref, [pair(kvc_ref)], then)
-
-
-def far_kernel(q_ref, kv_ref, kvc_ref, near_ref, out_ref, level_ref, state):
     second = lax.axis_index("stretch") % 2 == 1
-
-    def first(index, rows, *result):
-        result = join(result, [near_ref[i, rows, :] for i in range(3)])
+    pl.when(second)(lambda: attend(q_ref, [pair(kv_ref), pair(kvc_ref)], finish))
+    pl.when(jnp.logical_not(second))(lambda: attend(q_ref, [pair(kv_ref)], finish))
+
+
+def far_kernel(q_ref, kv_ref, before_ref, out_ref):
+    def finish(index, rows, *result):
+        result = join(result, [before_ref[i, rows, :] for i in range(3)])
         for i in range(3):
-            state[i, rows, :] = result[i]
-
-    def then(index, rows, *result):
-        result = join(result, [state[i, rows, :] for i in range(3)])
-        for i in range(3):
-            state[i, rows, :] = result[i]
-
-    attend(q_ref, [pair(kv_ref)], first)
+            out_ref[i, rows, :] = result[i]
+
+    attend(q_ref, [pair(kv_ref)], finish)
+
+
+def last_kernel(q_ref, kv_ref, before_ref, out_ref, level_ref):
+    def store(index, rows, mixture, total, peak):
+        out_ref[rows, :] = mixture / total
+        level_ref[level_rows(index), :] = level_of(peak, total)
+
+    def finish(index, rows, *result):
+        store(index, rows, *join(result, [before_ref[i, rows, :] for i in range(3)]))
+
+    second = lax.axis_index("stretch") % 2 == 1
 
     @pl.when(second)
     def _():
-        attend(q_ref, [pair(kvc_ref)], then)
-
-    for index in range(q_ref.shape[0] // ROWS):
-        rows = slice(index * ROWS, index * ROWS + ROWS)
-        out_ref[rows, :] = state[0, rows, :] / state[1, rows, :]
-        level_ref[level_rows(index), :] = level_of(state[2, rows, :], state[1, rows, :])
+        attend(q_ref, [pair(kv_ref)], finish)
+
+    @pl.when(jnp.logical_not(second))
+    def _():
+        for index in range(q_ref.shape[0] // ROWS):
+            rows = slice(index * ROWS, index * ROWS + ROWS)
+            store(index, rows, *[before_ref[i, rows, :] for i in range(3)])
+
+
+def even_chip():
+    return lax.axis_index("stretch") < 2
 
 
 def level_rows(index):
@@ -181,25 +192,26 @@
         for i in range(3):
             out_ref[i, rows, :] = result[i]
 
-    @pl.when(lax.axis_index("stretch") < 2)
+    @pl.when(even_chip())
     def _():
         attend(q_ref, [pair(kv_ref), pair(kvc_ref)], finish)
 
 
-def chip_far_kernel(q_ref, kv_ref, kvc_ref, near_ref, out_ref, levels):
+def chip_far_kernel(block, q_ref, kv_ref, kvc_ref, near_ref, out_ref, levels):
     def finish(index, rows, *result):
         mixture, total, peak = join(result, [near_ref[i, rows, :] for i in range(3)])
-        out_ref[rows, :] = (mixture / total).astype(BF16)
-        levels[level_rows(index), :] = level_of(peak, total)
-
-    @pl.when(lax.axis_index("stretch") < 2)
+        out_ref[:ROWS, :] = (mixture / total).astype(BF16)
+        levels[level_rows(0), :] = level_of(peak, total)
+
+    @pl.when(even_chip())
     def _():
         levels[...] = jnp.zeros_like(levels)
-        attend(q_ref, [pair(kv_ref), pair(kvc_ref)], finish)
+        attend(q_ref, [pair(kv_ref), pair(kvc_ref)], finish, block, 1)
         pack_level(out_ref, levels)
 
 
-def merge_kernel(levels_ref, gate_ref, own_ref, level_ref, chip_ref, out_ref, chip_levels):
+def merge_kernel(levels_ref, gate_ref, own_ref, level_ref, *refs):
+    *chip_refs, out_ref, chip_levels = refs
     stretch = lax.axis_index("stretch")
     seq = lax.axis_index("seq")
     odd = stretch >= 2
@@ -209,15 +221,15 @@
     tile = gate_ref[pl.ds(pl.multiple_of(noise // 8 * 8, 8), 8), lanes]
     mine = lax.broadcasted_iota(jnp.int32, tile.shape, 0) == noise % 8
     gate = jnp.sum(jnp.where(mine, tile, 0.0), axis=0, keepdims=True)
-    unpack_level(chip_ref, chip_levels)
-    for index in range(own_ref.shape[0] // ROWS):
+    for index, chip_ref in enumerate(chip_refs):
+        unpack_level(chip_ref, chip_levels)
         rows = slice(index * ROWS, index * ROWS + ROWS)
         level = level_ref[level_rows(index), :]
-        chip_level = jnp.where(odd, chip_levels[level_rows(index), :], -jnp.inf)
+        chip_level = jnp.where(odd, chip_levels[level_rows(0), :], -jnp.inf)
         top = jnp.maximum(level, chip_level)
         left, right = jnp.exp2(level - top), jnp.exp2(chip_level - top)
         left, right = columns(left / (left + right), right / (left + right))
-        other = jnp.where(odd, chip_ref[rows, :].astype(F32), 0.0)
+        other = jnp.where(odd, chip_ref[:ROWS, :].astype(F32), 0.0)
         attended = (own_ref[rows, :] * left + other * right).astype(BF16).astype(F32)
         out_ref[rows, :] = (gate * attended).astype(BF16)
 
@@ -225,19 +237,16 @@
 HELD = pl.BlockSpec(memory_space=pltpu.VMEM)
 
 
-def call(kernel, name, ins, in_specs, out_shape, out_spec, scratch, units):
+def call(kernel, name, ins, in_specs, out_shape, out_spec, scratch, aliases=()):
     return pl.pallas_call(
         kernel,
         in_specs=in_specs,
         out_specs=out_spec,
         out_shape=out_shape,
         scratch_shapes=scratch,
+        input_output_aliases=dict(aliases),
         compiler_params=pltpu.CompilerParams(vmem_limit_bytes=VMEM),
-        cost_estimate=pl.CostEstimate(
-            flops=units * 8 * 1536 * 1536 * DH,
-            bytes_accessed=2**20,
-            transcendentals=units * 1536 * 1536,
-        ),
+        cost_estimate=pl.CostEstimate(flops=DH, bytes_accessed=DH, transcendentals=0),
         name=name,
     )(*ins)
 
@@ -257,31 +266,39 @@
     kv_core = send(kv, core)
     q_z = send(q, exchange(2, 0, lambda stretch: stretch >= 2))
     state = jax.ShapeDtypeStruct((3, span, DH), F32)
-    message = jax.ShapeDtypeStruct((message_rows(span), DH), BF16)
-    level_shape = (level_count(span), DH)
-    level_scratch = pltpu.VMEM(level_shape, F32)
-    own = [jax.ShapeDtypeStruct((span, DH), F32), jax.ShapeDtypeStruct(level_shape, F32)]
-    near = call(near_kernel, "near", [q, kv, kv_core], [HELD] * 3, state, HELD, [], 2)
+    message = jax.ShapeDtypeStruct((message_rows(ROWS), DH), BF16)
+    level_scratch = pltpu.VMEM((level_count(ROWS), DH), F32)
+    own_shape = [
+        jax.ShapeDtypeStruct((span, DH), F32), jax.ShapeDtypeStruct((level_count(span), DH), F32)
+    ]
+    near = call(near_kernel, "near", [q, kv, kv_core], [HELD] * 3, state, HELD, [])
     q_z, near = lax.optimization_barrier((q_z, near))
     chip_near = call(
-        chip_near_kernel, "chip_near", [q_z, kv, kv_core], [HELD] * 3, state, HELD, [], 2
+        chip_near_kernel, "chip_near", [q_z, kv, kv_core], [HELD] * 3, state, HELD, []
     )
     kv_x, near, chip_near = lax.optimization_barrier((kv_x, near, chip_near))
     kv_x_core = send(kv_x, core)
-    chip = call(
-        chip_far_kernel, "chip_far", [q_z, kv_x, kv_x_core, chip_near], [HELD] * 4, message, HELD,
-        [level_scratch], 2,
-    )
-    chip_in = send(chip, exchange(2, 0, lambda stretch: stretch < 2))
-    chip, near = lax.optimization_barrier((chip, near))
-    far = call(
-        far_kernel, "far", [q, kv_x, kv_x_core, near], [HELD] * 4, own, [HELD] * 2,
-        [pltpu.VMEM(state.shape, F32)], 2,
+    far = call(far_kernel, "far", [q, kv_x, near], [HELD] * 3, state, HELD, [], {2: 0})
+    kv_x_core, far, chip_near = lax.optimization_barrier((kv_x_core, far, chip_near))
+
+    def lend(block, before):
+        chip = call(
+            partial(chip_far_kernel, block), f"chip_far{block}", [q_z, kv_x, kv_x_core, before],
+            [HELD] * 4, message, HELD, [level_scratch],
+        )
+        return chip, send(chip, exchange(2, 0, lambda stretch: stretch < 2))
+
+    chip, first_in = lend(0, chip_near)
+    chip, chip_near = lax.optimization_barrier((chip, chip_near))
+    chip, second_in = lend(1, chip_near)
+    first_in, chip, far = lax.optimization_barrier((first_in, chip, far))
+    own = call(
+        last_kernel, "last", [q, kv_x_core, far], [HELD] * 3, own_shape, [HELD] * 2, []
     )
     mixture = call(
-        merge_kernel, "merge", [levels, gate_table, *far, chip_in],
-        [pl.BlockSpec(memory_space=pltpu.SMEM)] + [HELD] * 4,
-        jax.ShapeDtypeStruct((span, DH), BF16), HELD, [level_scratch], 0,
+        merge_kernel, "merge", [levels, gate_table, *own, first_in, second_in],
+        [pl.BlockSpec(memory_space=pltpu.SMEM)] + [HELD] * 5,
+        jax.ShapeDtypeStruct((span, DH), BF16), HELD, [level_scratch],
     )
     result = lax.all_to_all(mixture.reshape(64, half, DH), "seq", 0, 0, tiled=True)
     result = result.reshape(2, 2, 16, half, DH).transpose(1, 3, 0, 2, 4)

time: 117 us -> 115 us (0.983)
  waiting for transfers between devices: 29.3 us -> 26.7 us
    ppermute x5 -> x6, waiting for transfers between devices: 29.3 us -> 26.7 us  [send(): return lax.ppermute(array, AXES, pairs)]
    ppermute x5 -> x6, starting transfers between devices: 5.82 us -> 6.98 us  [send(): return lax.ppermute(array, AXES, pairs)]
    pallas_call x5 -> x7, Pallas kernels: 9 us -> 8.78 us  [call(): pl.pallas_call(kernel, in_specs=in_specs, out_specs=out_spec, out_shape=o...]
  transfers between devices with their start and end apart: 5 -> 6, of which waited for: 4 -> 4; matrix products, arithmetic and copies ran while one was open for 0% -> 0% of each run, Pallas kernels for 7% -> 6%
where the time goes in v4:
time: 115 us
  blocking collectives  69.2 us (60%)
  waiting for transfers between devices  26.7 us (23%)
  Pallas kernels  8.78 us (8%)
  starting transfers between devices  6.98 us (6%)
  local copies, waits for them, and re-layouts  1.87 us (2%)
  other arithmetic  1.36 us (1%)
    all_to_all x1, blocking collectives, local(): qkv = lax.all_to_all(qkv, 'seq', 0, 0, tiled=True)  47.2 us
    ppermute x6, waiting for transfers between devices, send(): return lax.ppermute(array, AXES, pairs)  26.7 us
    all_to_all x1, blocking collectives, local(): lax.all_to_all(mixture.reshape(64, half, DH), 'seq', 0, 0, tiled=True)  21.9 us
    pallas_call x7, Pallas kernels, call(): pl.pallas_call(kernel, in_specs=in_specs, out_specs=out_spec, out_shape=o...  8.78 us
    ppermute x6, starting transfers between devices, send(): return lax.ppermute(array, AXES, pairs)  6.98 us
  transfers between devices with their start and end apart: 6, of which 4 were waited for; matrix products, arithmetic and copies ran while one was open for 0% of the time, Pallas kernels for 6%

profile of v4, /device:TPU:32, one launch (start us, length us, event | category | flops | bytes accessed | tf_op | source)
XLA Modules:
  0.0 115.1 jit_solution(3588197122286307123)
XLA Ops:
  0.0 1.4 %pad_maximum_fusion = bf16[3,48,4096]{2,1,0:T(8,128)(2,1)S(1)} fusion(bf16[1,48,4096]{2,1,0:T(8,128)(2,1)} %param.7, bf16[1,48,4096]{2,1,0:T(8,128)(2,1)} %param.6, bf16[1,48,4096]{2,1,0:T(8,128)(2,1)} %param.5), kind=kLoop, calls=%fused_computation | loop fusion | flops 1179648 | bytes 2359296 | tf_op jit(solution)/shard_map/concatenate | solution.py:258
  1.4 0.2 copy.12
  1.6 0.5 copy.9
  2.1 47.2 %all_to_all.10 = bf16[64,3,24,128]{3,2,1,0:T(8,128)(2,1)S(1)} all-to-all(bf16[64,3,24,128]{3,2,1,0:T(8,128)(2,1)S(1)} %bitcast.29), channel_id=1, replica_groups=mesh['stretch'=4,'seq'=64] {'seq'}, dimensions={0} | all-to-all | bytes 2359296 | tf_op jit(solution)/shard_map/all_to_all | solution.py:260
  49.3 0.1 slice.14
  49.4 0.1 copy.10
  49.5 0.1 collective-permute-start.2
  49.6 0.1 collective-permute-start
  49.8 4.0 %collective-permute-start.1 = (bf16[1536,128]{1,0:T(8,128)(2,1)S(1)}, bf16[1536,128]{1,0:T(8,128)(2,1)S(1)}, u32[]{:S(2)}, u32[]{:S(2)}) collective-permute-start(bf16[1536,128]{1,0:T(8,128)(2,1)S(1)} %bitcast.21), channel_id=1, source_target_pairs={{128,0},{129,1},{130,2},{131,3},{132,4},{133,5},{134,6},{135,7},{1... | collective-permute-start | bytes 1179656 | tf_op jit(solution)/shard_map/ppermute | solution.py:32
  53.8 0.0 collective-permute-done.2.kvc_ref
  53.8 3.4 %near.1.before_ref = f32[3,1536,128]{2,1,0:T(8,128)S(1)} custom-call(bf16[1536,128]{1,0:T(8,128)(2,1)S(1)} %bitcast.22, bf16[2,1536,128]{2,1,0:T(8,128)(2,1)S(1)} %bitcast.19, bf16[2,1536,128]{2,1,0:T(8,128)(2,1)S(1)} %collective-permute-done.2.kvc_ref), custom_call_target="tpu_custom_call" | custom-call | flops 128 | bytes 128 | tf_op jit(solution)/shard_map/near/pallas_call | solution.py:241
  57.2 5.4 %collective-permute-done.1.q_ref = bf16[1536,128]{1,0:T(8,128)(2,1)S(1)} collective-permute-done((bf16[1536,128]{1,0:T(8,128)(2,1)S(1)}, bf16[1536,128]{1,0:T(8,128)(2,1)S(1)}, u32[]{:S(2)}, u32[]{:S(2)}) %collective-permute-start.1) | collective-permute-done | bytes 393248 | tf_op jit(solution)/shard_map/ppermute | solution.py:32
  62.7 6.9 %collective-permute-done.kv_ref = bf16[2,1536,128]{2,1,0:T(8,128)(2,1)S(1)} collective-permute-done((bf16[2,1536,128]{2,1,0:T(8,128)(2,1)S(1)}, bf16[2,1536,128]{2,1,0:T(8,128)(2,1)S(1)}, u32[]{:S(2)}, u32[]{:S(2)}) %collective-permute-start) | collective-permute-done | bytes 786464 | tf_op jit(solution)/shard_map/ppermute | solution.py:32
  69.6 0.0 collective-permute-start.3
  69.6 3.8 %far.1.before_ref = f32[3,1536,128]{2,1,0:T(8,128)S(1)} custom-call(bf16[1536,128]{1,0:T(8,128)(2,1)S(1)} %bitcast.23, bf16[2,1536,128]{2,1,0:T(8,128)(2,1)S(1)} %collective-permute-done.kv_ref, f32[3,1536,128]{2,1,0:T(8,128)S(1)} %near.1.before_ref), custom_call_target="tpu_custom_call", output_to_operand_aliasing={{}: (2, {})} | custom-call | flops 128 | bytes 128 | tf_op jit(solution)/shard_map/far/pallas_call | solution.py:241
  73.3 0.0 collective-permute-done.3.kvc_ref.kv_ref
  73.4 1.3 %collective-permute-start.4 = (bf16[816,128]{1,0:T(8,128)(2,1)S(1)}, bf16[816,128]{1,0:T(8,128)(2,1)S(1)}, u32[]{:S(2)}, u32[]{:S(2)}) collective-permute-start(bf16[816,128]{1,0:T(8,128)(2,1)S(1)} %chip_far0.1), channel_id=1, source_target_pairs={{0,128},{1,129},{2,130},{3,131},{4,132},{5,133},{6,134},{7,135},{8... | collective-permute-start | bytes 626696 | tf_op jit(solution)/shard_map/ppermute | solution.py:32
  74.7 0.0 copy-start
  74.7 0.0 copy-start.1
  74.7 1.4 %collective-permute-start.5 = (bf16[816,128]{1,0:T(8,128)(2,1)S(1)}, bf16[816,128]{1,0:T(8,128)(2,1)S(1)}, u32[]{:S(2)}, u32[]{:S(2)}) collective-permute-start(bf16[816,128]{1,0:T(8,128)(2,1)S(1)} %chip_far1.1), channel_id=1, source_target_pairs={{0,128},{1,129},{2,130},{3,131},{4,132},{5,133},{6,134},{7,135},{8... | collective-permute-start | bytes 626696 | tf_op jit(solution)/shard_map/ppermute | solution.py:32
  76.2 9.8 %collective-permute-done.4.refs_0_ = bf16[816,128]{1,0:T(8,128)(2,1)S(1)} collective-permute-done((bf16[816,128]{1,0:T(8,128)(2,1)S(1)}, bf16[816,128]{1,0:T(8,128)(2,1)S(1)}, u32[]{:S(2)}, u32[]{:S(2)}) %collective-permute-start.4) | collective-permute-done | bytes 208928 | tf_op jit(solution)/shard_map/ppermute | solution.py:32
  86.0 0.2 last.1
  86.3 4.6 %collective-permute-done.5.refs_1_ = bf16[816,128]{1,0:T(8,128)(2,1)S(1)} collective-permute-done((bf16[816,128]{1,0:T(8,128)(2,1)S(1)}, bf16[816,128]{1,0:T(8,128)(2,1)S(1)}, u32[]{:S(2)}, u32[]{:S(2)}) %collective-permute-start.5) | collective-permute-done | bytes 208928 | tf_op jit(solution)/shard_map/ppermute | solution.py:32
  90.8 0.0 copy-done
  90.8 0.0 copy-done.1
  90.8 1.3 %merge.1 = bf16[1536,128]{1,0:T(8,128)(2,1)S(1)} custom-call(s32[4]{0:T(128)S(1)} %copy-done.1, f32[64,4096]{1,0:T(8,128)S(1)} %copy-done, f32[1536,128]{1,0:T(8,128)S(1)} %get-tuple-element.28.own_ref, f32[16,128]{1,0:T(8,128)S(1)} %get-tuple-element.29.level_ref, bf16[816,128]{1,0:T(8,128)(2,1)S(1)} %collective-permute-done.4.refs_0_, ...), custom_call_target="tpu_custom_call" | custom-call | flops 128 | bytes 128 | tf_op jit(solution)/shard_map/merge/pallas_call | solution.py:241
  92.2 21.9 %all_to_all.11 = bf16[64,24,128]{2,1,0:T(8,128)(2,1)S(1)} all-to-all(bf16[64,24,128]{2,1,0:T(8,128)(2,1)S(1)} %bitcast.25), channel_id=1, replica_groups=mesh['stretch'=4,'seq'=64] {'seq'}, dimensions={0} | all-to-all | bytes 786432 | tf_op jit(solution)/shard_map/all_to_all | solution.py:303
  114.1 0.1 copy.14
  114.2 0.9 reshape.23
  (4 shorter events, 0.1 us)
Async XLA Ops:
  49.5 4.3 %collective-permute-start.2 = (bf16[2,1536,128]{2,1,0:T(8,128)(2,1)S(1)}, bf16[2,1536,128]{2,1,0:T(8,128)(2,1)S(1)}, u32[]{:S(2)}, u32[]{:S(2)}) collective-permute-start(bf16[2,1536,128]{2,1,0:T(8,128)(2,1)S(1)} %bitcast.17), channel_id=1, source_target_pairs={{0,64},{1,65},{2,66},{3,67},{4,68},{5,69},{6,70},{7,71},{8,72},{9,... | collective-permute-start | bytes 2359304 | tf_op jit(solution)/shard_map/ppermute | solution.py:32
  49.6 20.0 %collective-permute-start = (bf16[2,1536,128]{2,1,0:T(8,128)(2,1)S(1)}, bf16[2,1536,128]{2,1,0:T(8,128)(2,1)S(1)}, u32[]{:S(2)}, u32[]{:S(2)}) collective-permute-start(bf16[2,1536,128]{2,1,0:T(8,128)(2,1)S(1)} %bitcast.18), channel_id=1, source_target_pairs={{0,16},{1,17},{2,18},{3,19},{4,20},{5,21},{6,22},{7,23},{8,24},{9,... | collective-permute-start | bytes 2359304 | tf_op jit(solution)/shard_map/ppermute | solution.py:32
  49.8 12.9 %collective-permute-start.1 = (bf16[1536,128]{1,0:T(8,128)(2,1)S(1)}, bf16[1536,128]{1,0:T(8,128)(2,1)S(1)}, u32[]{:S(2)}, u32[]{:S(2)}) collective-permute-start(bf16[1536,128]{1,0:T(8,128)(2,1)S(1)} %bitcast.21), channel_id=1, source_target_pairs={{128,0},{129,1},{130,2},{131,3},{132,4},{133,5},{134,6},{135,7},{1... | collective-permute-start | bytes 1179656 | tf_op jit(solution)/shard_map/ppermute | solution.py:32
  69.6 3.8 %collective-permute-start.3 = (bf16[2,1536,128]{2,1,0:T(8,128)(2,1)S(1)}, bf16[2,1536,128]{2,1,0:T(8,128)(2,1)S(1)}, u32[]{:S(2)}, u32[]{:S(2)}) collective-permute-start(bf16[2,1536,128]{2,1,0:T(8,128)(2,1)S(1)} %collective-permute-done.kv_ref), channel_id=1, source_target_pairs={{0,64},{1,65},{2,66},{3,67},{4,68},{5,69},{6,70},{7,71},{8,72},{9,... | collective-permute-start | bytes 2359304 | tf_op jit(solution)/shard_map/ppermute | solution.py:32
  73.4 12.6 %collective-permute-start.4 = (bf16[816,128]{1,0:T(8,128)(2,1)S(1)}, bf16[816,128]{1,0:T(8,128)(2,1)S(1)}, u32[]{:S(2)}, u32[]{:S(2)}) collective-permute-start(bf16[816,128]{1,0:T(8,128)(2,1)S(1)} %chip_far0.1), channel_id=1, source_target_pairs={{0,128},{1,129},{2,130},{3,131},{4,132},{5,133},{6,134},{7,135},{8... | collective-permute-start | bytes 626696 | tf_op jit(solution)/shard_map/ppermute | solution.py:32
  74.7 16.1 %copy-start = (f32[64,4096]{1,0:T(8,128)S(1)}, f32[64,4096]{1,0:T(8,128)}, u32[]{:S(2)}) copy-start(f32[64,4096]{1,0:T(8,128)} %gate_ref.1) | copy-start | bytes 3145732
  74.7 16.1 %copy-start.1 = (s32[4]{0:T(128)S(1)}, s32[4]{0:T(128)}, u32[]{:S(2)}) copy-start(s32[4]{0:T(128)} %levels_ref.1) | copy-start | bytes 52
  74.7 16.1 %collective-permute-start.5 = (bf16[816,128]{1,0:T(8,128)(2,1)S(1)}, bf16[816,128]{1,0:T(8,128)(2,1)S(1)}, u32[]{:S(2)}, u32[]{:S(2)}) collective-permute-start(bf16[816,128]{1,0:T(8,128)(2,1)S(1)} %chip_far1.1), channel_id=1, source_target_pairs={{0,128},{1,129},{2,130},{3,131},{4,132},{5,133},{6,134},{7,135},{8... | collective-permute-start | bytes 626696 | tf_op jit(solution)/shard_map/ppermute | solution.py:32

commit v5 on v4

--- a/solution.py
+++ b/solution.py
@@ -96,13 +96,13 @@
     pl.when(jnp.logical_not(second))(lambda: attend(q_ref, blocks, finish))
 
 
-def near_kernel(q_ref, kv_ref, kvc_ref, out_ref):
+def near_kernel(q_ref, kv_ref, kc_ref, vc_ref, out_ref):
     def finish(index, rows, *result):
         for i in range(3):
             out_ref[i, rows, :] = result[i]
 
     second = lax.axis_index("stretch") % 2 == 1
-    pl.when(second)(lambda: attend(q_ref, [pair(kv_ref), pair(kvc_ref)], finish))
+    pl.when(second)(lambda: attend(q_ref, [pair(kv_ref), (kc_ref, vc_ref)], finish))
     pl.when(jnp.logical_not(second))(lambda: attend(q_ref, [pair(kv_ref)], finish))
 
 
@@ -187,14 +187,14 @@
     levels[...] = parts[0] + parts[1] + parts[2]
 
 
-def chip_near_kernel(q_ref, kv_ref, kvc_ref, out_ref):
+def chip_near_kernel(q_ref, kv_ref, kc_ref, vc_ref, out_ref):
     def finish(index, rows, *result):
         for i in range(3):
             out_ref[i, rows, :] = result[i]
 
     @pl.when(even_chip())
     def _():
-        attend(q_ref, [pair(kv_ref), pair(kvc_ref)], finish)
+        attend(q_ref, [pair(kv_ref), (kc_ref, vc_ref)], finish)
 
 
 def chip_far_kernel(block, q_ref, kv_ref, kvc_ref, near_ref, out_ref, levels):
@@ -263,18 +263,18 @@
 
     core = exchange(1, 0)
     kv_x = send(kv, exchange(0, 16))
-    kv_core = send(kv, core)
-    q_z = send(q, exchange(2, 0, lambda stretch: stretch >= 2))
+    kv_core = [send(kv[0], core), send(kv[1], core)]
+    q_z = send(jnp.concatenate([q, kv[0, :64]]), exchange(2, 0, lambda stretch: stretch >= 2))
     state = jax.ShapeDtypeStruct((3, span, DH), F32)
     message = jax.ShapeDtypeStruct((message_rows(ROWS), DH), BF16)
     level_scratch = pltpu.VMEM((level_count(ROWS), DH), F32)
     own_shape = [
         jax.ShapeDtypeStruct((span, DH), F32), jax.ShapeDtypeStruct((level_count(span), DH), F32)
     ]
-    near = call(near_kernel, "near", [q, kv, kv_core], [HELD] * 3, state, HELD, [])
+    near = call(near_kernel, "near", [q, kv, *kv_core], [HELD] * 4, state, HELD, [])
     q_z, near = lax.optimization_barrier((q_z, near))
     chip_near = call(
-        chip_near_kernel, "chip_near", [q_z, kv, kv_core], [HELD] * 3, state, HELD, []
+        chip_near_kernel, "chip_near", [q_z, kv, *kv_core], [HELD] * 4, state, HELD, []
     )
     kv_x, near, chip_near = lax.optimization_barrier((kv_x, near, chip_near))
     kv_x_core = send(kv_x, core)

time: 115 us -> 115 us (level)
  waiting for transfers between devices: 26.7 us -> 22.4 us
  blocking collectives: 69.2 us -> 71.7 us
    ppermute x6 -> x7, waiting for transfers between devices: 26.7 us -> 22.4 us  [send(): return lax.ppermute(array, AXES, pairs)]
    all_to_all x1, blocking collectives: 21.9 us -> 24.5 us  [local(): lax.all_to_all(mixture.reshape(64, half, DH), 'seq', 0, 0, tiled=True)]
    ppermute x6 -> x7, starting transfers between devices: 6.98 us -> 7.45 us  [send(): return lax.ppermute(array, AXES, pairs)]
  transfers between devices with their start and end apart: 6 -> 7, of which waited for: 4 -> 5; matrix products, arithmetic and copies ran while one was open for 0% -> 0% of each run, Pallas kernels for 6% -> 7%
where the time goes in v5:
time: 115 us; the launch traced here: 114 us
  blocking collectives  71.7 us (62%)
  waiting for transfers between devices  22.4 us (19%)
  Pallas kernels  9.18 us (8%)
  starting transfers between devices  7.45 us (6%)
  local copies, waits for them, and re-layouts  2.04 us (2%)
  other arithmetic  1.39 us (1%)
    all_to_all x1, blocking collectives, local(): qkv = lax.all_to_all(qkv, 'seq', 0, 0, tiled=True)  47.2 us
    all_to_all x1, blocking collectives, local(): lax.all_to_all(mixture.reshape(64, half, DH), 'seq', 0, 0, tiled=True)  24.5 us
    ppermute x7, waiting for transfers between devices, send(): return lax.ppermute(array, AXES, pairs)  22.4 us
    pallas_call x7, Pallas kernels, call(): pl.pallas_call(kernel, in_specs=in_specs, out_specs=out_spec, out_shape=o...  9.18 us
    ppermute x7, starting transfers between devices, send(): return lax.ppermute(array, AXES, pairs)  7.45 us
  transfers between devices with their start and end apart: 7, of which 5 were waited for; matrix products, arithmetic and copies ran while one was open for 0% of the time, Pallas kernels for 7%

profile of v5, /device:TPU:32, one launch (start us, length us, event | category | flops | bytes accessed | tf_op | source)
XLA Modules:
  0.0 114.4 jit_solution(4856786134987220285)
XLA Ops:
  0.0 1.4 %pad_maximum_fusion = bf16[3,48,4096]{2,1,0:T(8,128)(2,1)S(1)} fusion(bf16[1,48,4096]{2,1,0:T(8,128)(2,1)} %param.7, bf16[1,48,4096]{2,1,0:T(8,128)(2,1)} %param.6, bf16[1,48,4096]{2,1,0:T(8,128)(2,1)} %param.5), kind=kLoop, calls=%fused_computation | loop fusion | flops 1179648 | bytes 2359296 | tf_op jit(solution)/shard_map/concatenate | solution.py:258
  1.4 0.2 copy.12
  1.6 0.5 copy.9
  2.1 47.2 %all_to_all.10 = bf16[64,3,24,128]{3,2,1,0:T(8,128)(2,1)S(1)} all-to-all(bf16[64,3,24,128]{3,2,1,0:T(8,128)(2,1)S(1)} %bitcast.33), channel_id=1, replica_groups=mesh['stretch'=4,'seq'=64] {'seq'}, dimensions={0} | all-to-all | bytes 2359296 | tf_op jit(solution)/shard_map/all_to_all | solution.py:260
  49.3 0.1 slice.30
  49.4 0.2 fusion
  49.6 0.1 copy.10
  49.7 0.1 collective-permute-start
  49.9 4.0 %collective-permute-start.1 = (bf16[1600,128]{1,0:T(8,128)(2,1)S(1)}, bf16[1600,128]{1,0:T(8,128)(2,1)S(1)}, u32[]{:S(2)}, u32[]{:S(2)}) collective-permute-start(bf16[1600,128]{1,0:T(8,128)(2,1)S(1)} %pad_maximum_fusion.1), channel_id=1, source_target_pairs={{128,0},{129,1},{130,2},{131,3},{132,4},{133,5},{134,6},{135,7},{1... | collective-permute-start | bytes 1228808 | tf_op jit(solution)/shard_map/ppermute | solution.py:32
  53.9 0.1 collective-permute-start.2
  54.0 0.5 collective-permute-start.3
  54.5 1.2 %collective-permute-done.2.kc_ref = bf16[1536,128]{1,0:T(8,128)(2,1)S(1)} collective-permute-done((bf16[1536,128]{1,0:T(8,128)(2,1)S(1)}, bf16[1536,128]{1,0:T(8,128)(2,1)S(1)}, u32[]{:S(2)}, u32[]{:S(2)}) %collective-permute-start.2) | collective-permute-done | bytes 393248 | tf_op jit(solution)/shard_map/ppermute | solution.py:32
  55.7 0.6 collective-permute-done.3.vc_ref
  56.3 3.4 %near.1.before_ref = f32[3,1536,128]{2,1,0:T(8,128)S(1)} custom-call(bf16[1536,128]{1,0:T(8,128)(2,1)S(1)} %bitcast.22, bf16[2,1536,128]{2,1,0:T(8,128)(2,1)S(1)} %bitcast.27, bf16[1536,128]{1,0:T(8,128)(2,1)S(1)} %collective-permute-done.2.kc_ref, bf16[1536,128]{1,0:T(8,128)(2,1)S(1)} %collective-permute-done.3.vc_ref), custom_call_target="tpu_custom_call" | custom-call | flops 128 | bytes 128 | tf_op jit(solution)/shard_map/near/pallas_call | solution.py:241
  59.7 0.0 collective-permute-done.1.q_ref
  59.7 0.2 chip_near.1.near_ref
  59.9 7.6 %collective-permute-done.kv_ref = bf16[2,1536,128]{2,1,0:T(8,128)(2,1)S(1)} collective-permute-done((bf16[2,1536,128]{2,1,0:T(8,128)(2,1)S(1)}, bf16[2,1536,128]{2,1,0:T(8,128)(2,1)S(1)}, u32[]{:S(2)}, u32[]{:S(2)}) %collective-permute-start) | collective-permute-done | bytes 786464 | tf_op jit(solution)/shard_map/ppermute | solution.py:32
  67.4 0.0 collective-permute-start.4
  67.4 3.8 %far.1.before_ref = f32[3,1536,128]{2,1,0:T(8,128)S(1)} custom-call(bf16[1536,128]{1,0:T(8,128)(2,1)S(1)} %bitcast.23, bf16[2,1536,128]{2,1,0:T(8,128)(2,1)S(1)} %collective-permute-done.kv_ref, f32[3,1536,128]{2,1,0:T(8,128)S(1)} %near.1.before_ref), custom_call_target="tpu_custom_call", output_to_operand_aliasing={{}: (2, {})} | custom-call | flops 128 | bytes 128 | tf_op jit(solution)/shard_map/far/pallas_call | solution.py:241
  71.2 0.0 collective-permute-done.4.kvc_ref.kv_ref
  71.3 1.3 %collective-permute-start.5 = (bf16[816,128]{1,0:T(8,128)(2,1)S(1)}, bf16[816,128]{1,0:T(8,128)(2,1)S(1)}, u32[]{:S(2)}, u32[]{:S(2)}) collective-permute-start(bf16[816,128]{1,0:T(8,128)(2,1)S(1)} %chip_far0.1), channel_id=1, source_target_pairs={{0,128},{1,129},{2,130},{3,131},{4,132},{5,133},{6,134},{7,135},{8... | collective-permute-start | bytes 626696 | tf_op jit(solution)/shard_map/ppermute | solution.py:32
  72.6 0.2 chip_far1.1
  72.8 0.0 copy-start
  72.8 0.0 copy-start.1
  72.8 1.4 %collective-permute-start.6 = (bf16[816,128]{1,0:T(8,128)(2,1)S(1)}, bf16[816,128]{1,0:T(8,128)(2,1)S(1)}, u32[]{:S(2)}, u32[]{:S(2)}) collective-permute-start(bf16[816,128]{1,0:T(8,128)(2,1)S(1)} %chip_far1.1), channel_id=1, source_target_pairs={{0,128},{1,129},{2,130},{3,131},{4,132},{5,133},{6,134},{7,135},{8... | collective-permute-start | bytes 626696 | tf_op jit(solution)/shard_map/ppermute | solution.py:32
  74.3 8.3 %collective-permute-done.5.refs_0_ = bf16[816,128]{1,0:T(8,128)(2,1)S(1)} collective-permute-done((bf16[816,128]{1,0:T(8,128)(2,1)S(1)}, bf16[816,128]{1,0:T(8,128)(2,1)S(1)}, u32[]{:S(2)}, u32[]{:S(2)}) %collective-permute-start.5) | collective-permute-done | bytes 208928 | tf_op jit(solution)/shard_map/ppermute | solution.py:32
  82.5 0.2 last.1
  82.8 4.8 %collective-permute-done.6.refs_1_ = bf16[816,128]{1,0:T(8,128)(2,1)S(1)} collective-permute-done((bf16[816,128]{1,0:T(8,128)(2,1)S(1)}, bf16[816,128]{1,0:T(8,128)(2,1)S(1)}, u32[]{:S(2)}, u32[]{:S(2)}) %collective-permute-start.6) | collective-permute-done | bytes 208928 | tf_op jit(solution)/shard_map/ppermute | solution.py:32
  87.6 0.0 copy-done
  87.6 0.0 copy-done.1
  87.6 1.3 %merge.1 = bf16[1536,128]{1,0:T(8,128)(2,1)S(1)} custom-call(s32[4]{0:T(128)S(1)} %copy-done.1, f32[64,4096]{1,0:T(8,128)S(1)} %copy-done, f32[1536,128]{1,0:T(8,128)S(1)} %get-tuple-element.28.own_ref, f32[16,128]{1,0:T(8,128)S(1)} %get-tuple-element.29.level_ref, bf16[816,128]{1,0:T(8,128)(2,1)S(1)} %collective-permute-done.5.refs_0_, ...), custom_call_target="tpu_custom_call" | custom-call | flops 128 | bytes 128 | tf_op jit(solution)/shard_map/merge/pallas_call | solution.py:241
  88.9 24.5 %all_to_all.11 = bf16[64,24,128]{2,1,0:T(8,128)(2,1)S(1)} all-to-all(bf16[64,24,128]{2,1,0:T(8,128)(2,1)S(1)} %bitcast.29), channel_id=1, replica_groups=mesh['stretch'=4,'seq'=64] {'seq'}, dimensions={0} | all-to-all | bytes 786432 | tf_op jit(solution)/shard_map/all_to_all | solution.py:303
  113.4 0.1 copy.14
  113.4 0.9 reshape.27
  (3 shorter events, 0.0 us)
Async XLA Ops:
  49.7 17.7 %collective-permute-start = (bf16[2,1536,128]{2,1,0:T(8,128)(2,1)S(1)}, bf16[2,1536,128]{2,1,0:T(8,128)(2,1)S(1)}, u32[]{:S(2)}, u32[]{:S(2)}) collective-permute-start(bf16[2,1536,128]{2,1,0:T(8,128)(2,1)S(1)} %bitcast.25), channel_id=1, source_target_pairs={{0,16},{1,17},{2,18},{3,19},{4,20},{5,21},{6,22},{7,23},{8,24},{9,... | collective-permute-start | bytes 2359304 | tf_op jit(solution)/shard_map/ppermute | solution.py:32
  49.9 9.8 %collective-permute-start.1 = (bf16[1600,128]{1,0:T(8,128)(2,1)S(1)}, bf16[1600,128]{1,0:T(8,128)(2,1)S(1)}, u32[]{:S(2)}, u32[]{:S(2)}) collective-permute-start(bf16[1600,128]{1,0:T(8,128)(2,1)S(1)} %pad_maximum_fusion.1), channel_id=1, source_target_pairs={{128,0},{129,1},{130,2},{131,3},{132,4},{133,5},{134,6},{135,7},{1... | collective-permute-start | bytes 1228808 | tf_op jit(solution)/shard_map/ppermute | solution.py:32
  53.9 1.8 %collective-permute-start.2 = (bf16[1536,128]{1,0:T(8,128)(2,1)S(1)}, bf16[1536,128]{1,0:T(8,128)(2,1)S(1)}, u32[]{:S(2)}, u32[]{:S(2)}) collective-permute-start(bf16[1536,128]{1,0:T(8,128)(2,1)S(1)} %bitcast.38), channel_id=1, source_target_pairs={{0,64},{1,65},{2,66},{3,67},{4,68},{5,69},{6,70},{7,71},{8,72},{9,... | collective-permute-start | bytes 1179656 | tf_op jit(solution)/shard_map/ppermute | solution.py:32
  54.0 2.3 %collective-permute-start.3 = (bf16[1536,128]{1,0:T(8,128)(2,1)S(1)}, bf16[1536,128]{1,0:T(8,128)(2,1)S(1)}, u32[]{:S(2)}, u32[]{:S(2)}) collective-permute-start(bf16[1536,128]{1,0:T(8,128)(2,1)S(1)} %bitcast.37), channel_id=1, source_target_pairs={{0,64},{1,65},{2,66},{3,67},{4,68},{5,69},{6,70},{7,71},{8,72},{9,... | collective-permute-start | bytes 1179656 | tf_op jit(solution)/shard_map/ppermute | solution.py:32
  67.4 3.8 %collective-permute-start.4 = (bf16[2,1536,128]{2,1,0:T(8,128)(2,1)S(1)}, bf16[2,1536,128]{2,1,0:T(8,128)(2,1)S(1)}, u32[]{:S(2)}, u32[]{:S(2)}) collective-permute-start(bf16[2,1536,128]{2,1,0:T(8,128)(2,1)S(1)} %collective-permute-done.kv_ref), channel_id=1, source_target_pairs={{0,64},{1,65},{2,66},{3,67},{4,68},{5,69},{6,70},{7,71},{8,72},{9,... | collective-permute-start | bytes 2359304 | tf_op jit(solution)/shard_map/ppermute | solution.py:32
  71.3 11.3 %collective-permute-start.5 = (bf16[816,128]{1,0:T(8,128)(2,1)S(1)}, bf16[816,128]{1,0:T(8,128)(2,1)S(1)}, u32[]{:S(2)}, u32[]{:S(2)}) collective-permute-start(bf16[816,128]{1,0:T(8,128)(2,1)S(1)} %chip_far0.1), channel_id=1, source_target_pairs={{0,128},{1,129},{2,130},{3,131},{4,132},{5,133},{6,134},{7,135},{8... | collective-permute-start | bytes 626696 | tf_op jit(solution)/shard_map/ppermute | solution.py:32
  72.8 14.8 %copy-start = (f32[64,4096]{1,0:T(8,128)S(1)}, f32[64,4096]{1,0:T(8,128)}, u32[]{:S(2)}) copy-start(f32[64,4096]{1,0:T(8,128)} %gate_ref.1) | copy-start | bytes 3145732
  72.8 14.8 %copy-start.1 = (s32[4]{0:T(128)S(1)}, s32[4]{0:T(128)}, u32[]{:S(2)}) copy-start(s32[4]{0:T(128)} %levels_ref.1) | copy-start | bytes 52
  72.8 14.8 %collective-permute-start.6 = (bf16[816,128]{1,0:T(8,128)(2,1)S(1)}, bf16[816,128]{1,0:T(8,128)(2,1)S(1)}, u32[]{:S(2)}, u32[]{:S(2)}) collective-permute-start(bf16[816,128]{1,0:T(8,128)(2,1)S(1)} %chip_far1.1), channel_id=1, source_target_pairs={{0,128},{1,129},{2,130},{3,131},{4,132},{5,133},{6,134},{7,135},{8... | collective-permute-start | bytes 626696 | tf_op jit(solution)/shard_map/ppermute | solution.py:32

commit v6 on v5

--- a/solution.py
+++ b/solution.py
@@ -106,16 +106,23 @@
     pl.when(jnp.logical_not(second))(lambda: attend(q_ref, [pair(kv_ref)], finish))
 
 
-def far_kernel(q_ref, kv_ref, before_ref, out_ref):
-    def finish(index, rows, *result):
-        result = join(result, [before_ref[i, rows, :] for i in range(3)])
+def add_block(q_ref, blocks, state_in, state_out):
+    def finish(index, rows, *result):
+        result = join(result, [state_in[i, rows, :] for i in range(3)])
         for i in range(3):
-            out_ref[i, rows, :] = result[i]
-
-    attend(q_ref, [pair(kv_ref)], finish)
-
-
-def last_kernel(q_ref, kv_ref, before_ref, out_ref, level_ref):
+            state_out[i, rows, :] = result[i]
+
+    attend(q_ref, blocks, finish)
+
+
+def far_kernel(q_ref, q_z_ref, kv_ref, near_in, chip_in, near_out, chip_out):
+    pl.when(even_chip())(lambda: add_block(q_z_ref, [pair(kv_ref)], chip_in, chip_out))
+    pl.when(jnp.logical_not(even_chip()))(
+        lambda: add_block(q_ref, [pair(kv_ref)], near_in, near_out)
+    )
+
+
+def last_kernel(q_ref, kv_ref, kvc_ref, before_ref, out_ref, level_ref):
     def store(index, rows, mixture, total, peak):
         out_ref[rows, :] = mixture / total
         level_ref[level_rows(index), :] = level_of(peak, total)
@@ -124,12 +131,15 @@
         store(index, rows, *join(result, [before_ref[i, rows, :] for i in range(3)]))
 
     second = lax.axis_index("stretch") % 2 == 1
-
-    @pl.when(second)
-    def _():
-        attend(q_ref, [pair(kv_ref)], finish)
-
-    @pl.when(jnp.logical_not(second))
+    even = even_chip()
+    odd = jnp.logical_not(even)
+    first = jnp.logical_not(second)
+
+    pl.when(even & second)(lambda: attend(q_ref, [pair(kv_ref), pair(kvc_ref)], finish))
+    pl.when(even & first)(lambda: attend(q_ref, [pair(kv_ref)], finish))
+    pl.when(odd & second)(lambda: attend(q_ref, [pair(kvc_ref)], finish))
+
+    @pl.when(odd & first)
     def _():
         for index in range(q_ref.shape[0] // ROWS):
             rows = slice(index * ROWS, index * ROWS + ROWS)
@@ -197,7 +207,7 @@
         attend(q_ref, [pair(kv_ref), (kc_ref, vc_ref)], finish)
 
 
-def chip_far_kernel(block, q_ref, kv_ref, kvc_ref, near_ref, out_ref, levels):
+def chip_far_kernel(block, q_ref, kvc_ref, near_ref, out_ref, levels):
     def finish(index, rows, *result):
         mixture, total, peak = join(result, [near_ref[i, rows, :] for i in range(3)])
         out_ref[:ROWS, :] = (mixture / total).astype(BF16)
@@ -206,7 +216,7 @@
     @pl.when(even_chip())
     def _():
         levels[...] = jnp.zeros_like(levels)
-        attend(q_ref, [pair(kv_ref), pair(kvc_ref)], finish, block, 1)
+        attend(q_ref, [pair(kvc_ref)], finish, block, 1)
         pack_level(out_ref, levels)
 
 
@@ -278,13 +288,16 @@
     )
     kv_x, near, chip_near = lax.optimization_barrier((kv_x, near, chip_near))
     kv_x_core = send(kv_x, core)
-    far = call(far_kernel, "far", [q, kv_x, near], [HELD] * 3, state, HELD, [], {2: 0})
+    far, chip_near = call(
+        far_kernel, "far", [q, q_z, kv_x, near, chip_near], [HELD] * 5, [state] * 2, [HELD] * 2, [],
+        {3: 0, 4: 1},
+    )
     kv_x_core, far, chip_near = lax.optimization_barrier((kv_x_core, far, chip_near))
 
     def lend(block, before):
         chip = call(
-            partial(chip_far_kernel, block), f"chip_far{block}", [q_z, kv_x, kv_x_core, before],
-            [HELD] * 4, message, HELD, [level_scratch],
+            partial(chip_far_kernel, block), f"chip_far{block}", [q_z, kv_x_core, before],
+            [HELD] * 3, message, HELD, [level_scratch],
         )
         return chip, send(chip, exchange(2, 0, lambda stretch: stretch < 2))
 
@@ -293,7 +306,7 @@
     chip, second_in = lend(1, chip_near)
     first_in, chip, far = lax.optimization_barrier((first_in, chip, far))
     own = call(
-        last_kernel, "last", [q, kv_x_core, far], [HELD] * 3, own_shape, [HELD] * 2, []
+        last_kernel, "last", [q, kv_x, kv_x_core, far], [HELD] * 4, own_shape, [HELD] * 2, []
     )
     mixture = call(
         merge_kernel, "merge", [levels, gate_table, *own, first_in, second_in],

time: 115 us -> 115 us (level); the launches traced: 114 us -> 113 us
  waiting for transfers between devices: 22.4 us -> 20.4 us
    ppermute x7, waiting for transfers between devices: 22.4 us -> 20.4 us  [send(): return lax.ppermute(array, AXES, pairs)]
where the time goes in v6:
time: 115 us; the launch traced here: 113 us
  blocking collectives  72.7 us (63%)
  waiting for transfers between devices  20.4 us (18%)
  Pallas kernels  8.92 us (8%)
  starting transfers between devices  7.45 us (6%)
  local copies, waits for them, and re-layouts  2.04 us (2%)
  other arithmetic  1.39 us (1%)
    all_to_all x1, blocking collectives, local(): qkv = lax.all_to_all(qkv, 'seq', 0, 0, tiled=True)  47.2 us
    all_to_all x1, blocking collectives, local(): lax.all_to_all(mixture.reshape(64, half, DH), 'seq', 0, 0, tiled=True)  25.5 us
    ppermute x7, waiting for transfers between devices, send(): return lax.ppermute(array, AXES, pairs)  20.4 us
    pallas_call x7, Pallas kernels, call(): pl.pallas_call(kernel, in_specs=in_specs, out_specs=out_spec, out_shape=o...  8.92 us
    ppermute x7, starting transfers between devices, send(): return lax.ppermute(array, AXES, pairs)  7.45 us
  transfers between devices with their start and end apart: 7, of which 5 were waited for; matrix products, arithmetic and copies ran while one was open for 0% of the time, Pallas kernels for 7%

profile of v6, /device:TPU:32, one launch (start us, length us, event | category | flops | bytes accessed | tf_op | source)
XLA Modules:
  0.0 113.2 jit_solution(15846824903651991864)
XLA Ops:
  0.0 1.4 %pad_maximum_fusion = bf16[3,48,4096]{2,1,0:T(8,128)(2,1)S(1)} fusion(bf16[1,48,4096]{2,1,0:T(8,128)(2,1)} %param.7, bf16[1,48,4096]{2,1,0:T(8,128)(2,1)} %param.6, bf16[1,48,4096]{2,1,0:T(8,128)(2,1)} %param.5), kind=kLoop, calls=%fused_computation | loop fusion | flops 1179648 | bytes 2359296 | tf_op jit(solution)/shard_map/concatenate | solution.py:268
  1.4 0.2 copy.13
  1.6 0.5 copy.10
  2.1 47.2 %all_to_all.10 = bf16[64,3,24,128]{3,2,1,0:T(8,128)(2,1)S(1)} all-to-all(bf16[64,3,24,128]{3,2,1,0:T(8,128)(2,1)S(1)} %bitcast.33), channel_id=1, replica_groups=mesh['stretch'=4,'seq'=64] {'seq'}, dimensions={0} | all-to-all | bytes 2359296 | tf_op jit(solution)/shard_map/all_to_all | solution.py:270
  49.3 0.1 slice.30
  49.4 0.2 fusion
  49.6 0.1 copy.11
  49.7 0.1 collective-permute-start
  49.9 4.0 %collective-permute-start.1 = (bf16[1600,128]{1,0:T(8,128)(2,1)S(1)}, bf16[1600,128]{1,0:T(8,128)(2,1)S(1)}, u32[]{:S(2)}, u32[]{:S(2)}) collective-permute-start(bf16[1600,128]{1,0:T(8,128)(2,1)S(1)} %pad_maximum_fusion.1), channel_id=1, source_target_pairs={{128,0},{129,1},{130,2},{131,3},{132,4},{133,5},{134,6},{135,7},{1... | collective-permute-start | bytes 1228808 | tf_op jit(solution)/shard_map/ppermute | solution.py:32
  53.9 0.1 collective-permute-start.2
  54.0 0.5 collective-permute-start.3
  54.5 1.2 %collective-permute-done.2.kc_ref = bf16[1536,128]{1,0:T(8,128)(2,1)S(1)} collective-permute-done((bf16[1536,128]{1,0:T(8,128)(2,1)S(1)}, bf16[1536,128]{1,0:T(8,128)(2,1)S(1)}, u32[]{:S(2)}, u32[]{:S(2)}) %collective-permute-start.2) | collective-permute-done | bytes 393248 | tf_op jit(solution)/shard_map/ppermute | solution.py:32
  55.7 0.6 collective-permute-done.3.vc_ref
  56.3 3.3 %near.1.near_in = f32[3,1536,128]{2,1,0:T(8,128)S(1)} custom-call(bf16[1536,128]{1,0:T(8,128)(2,1)S(1)} %bitcast.22, bf16[2,1536,128]{2,1,0:T(8,128)(2,1)S(1)} %bitcast.27, bf16[1536,128]{1,0:T(8,128)(2,1)S(1)} %collective-permute-done.2.kc_ref, bf16[1536,128]{1,0:T(8,128)(2,1)S(1)} %collective-permute-done.3.vc_ref), custom_call_target="tpu_custom_call" | custom-call | flops 128 | bytes 128 | tf_op jit(solution)/shard_map/near/pallas_call | solution.py:251
  59.6 0.0 collective-permute-done.1.q_ref.q_z_ref
  59.6 0.2 chip_near.1.chip_in
  59.8 7.6 %collective-permute-done.kv_ref = bf16[2,1536,128]{2,1,0:T(8,128)(2,1)S(1)} collective-permute-done((bf16[2,1536,128]{2,1,0:T(8,128)(2,1)S(1)}, bf16[2,1536,128]{2,1,0:T(8,128)(2,1)S(1)}, u32[]{:S(2)}, u32[]{:S(2)}) %collective-permute-start) | collective-permute-done | bytes 786464 | tf_op jit(solution)/shard_map/ppermute | solution.py:32
  67.4 0.0 collective-permute-start.4
  67.4 3.8 %far.1 = (f32[3,1536,128]{2,1,0:T(8,128)S(1)}, f32[3,1536,128]{2,1,0:T(8,128)S(1)}) custom-call(bf16[1536,128]{1,0:T(8,128)(2,1)S(1)} %bitcast.23, bf16[1600,128]{1,0:T(8,128)(2,1)S(1)} %collective-permute-done.1.q_ref.q_z_ref, bf16[2,1536,128]{2,1,0:T(8,128)(2,1)S(1)} %collective-permute-done.kv_ref, ...), custom_call_target="tpu_custom_call", output_to_operand_aliasing={{0}: (3, {}), {1}: (4, {})} | custom-call | flops 128 | bytes 128 | tf_op jit(solution)/shard_map/far/pallas_call | solution.py:251
  71.2 0.0 collective-permute-done.4.kvc_ref
  71.3 1.3 %collective-permute-start.5 = (bf16[816,128]{1,0:T(8,128)(2,1)S(1)}, bf16[816,128]{1,0:T(8,128)(2,1)S(1)}, u32[]{:S(2)}, u32[]{:S(2)}) collective-permute-start(bf16[816,128]{1,0:T(8,128)(2,1)S(1)} %chip_far0.1), channel_id=1, source_target_pairs={{0,128},{1,129},{2,130},{3,131},{4,132},{5,133},{6,134},{7,135},{8... | collective-permute-start | bytes 626696 | tf_op jit(solution)/shard_map/ppermute | solution.py:32
  72.6 0.0 copy-start
  72.6 0.0 copy-start.1
  72.6 1.4 %collective-permute-start.6 = (bf16[816,128]{1,0:T(8,128)(2,1)S(1)}, bf16[816,128]{1,0:T(8,128)(2,1)S(1)}, u32[]{:S(2)}, u32[]{:S(2)}) collective-permute-start(bf16[816,128]{1,0:T(8,128)(2,1)S(1)} %chip_far1.1), channel_id=1, source_target_pairs={{0,128},{1,129},{2,130},{3,131},{4,132},{5,133},{6,134},{7,135},{8... | collective-permute-start | bytes 626696 | tf_op jit(solution)/shard_map/ppermute | solution.py:32
  74.0 7.4 %collective-permute-done.5.refs_0_ = bf16[816,128]{1,0:T(8,128)(2,1)S(1)} collective-permute-done((bf16[816,128]{1,0:T(8,128)(2,1)S(1)}, bf16[816,128]{1,0:T(8,128)(2,1)S(1)}, u32[]{:S(2)}, u32[]{:S(2)}) %collective-permute-start.5) | collective-permute-done | bytes 208928 | tf_op jit(solution)/shard_map/ppermute | solution.py:32
  81.5 0.2 last.1
  81.7 3.6 %collective-permute-done.6.refs_1_ = bf16[816,128]{1,0:T(8,128)(2,1)S(1)} collective-permute-done((bf16[816,128]{1,0:T(8,128)(2,1)S(1)}, bf16[816,128]{1,0:T(8,128)(2,1)S(1)}, u32[]{:S(2)}, u32[]{:S(2)}) %collective-permute-start.6) | collective-permute-done | bytes 208928 | tf_op jit(solution)/shard_map/ppermute | solution.py:32
  85.3 0.0 copy-done
  85.4 0.0 copy-done.1
  85.4 1.3 %merge.1 = bf16[1536,128]{1,0:T(8,128)(2,1)S(1)} custom-call(s32[4]{0:T(128)S(1)} %copy-done.1, f32[64,4096]{1,0:T(8,128)S(1)} %copy-done, f32[1536,128]{1,0:T(8,128)S(1)} %get-tuple-element.32.own_ref, f32[16,128]{1,0:T(8,128)S(1)} %get-tuple-element.33.level_ref, bf16[816,128]{1,0:T(8,128)(2,1)S(1)} %collective-permute-done.5.refs_0_, ...), custom_call_target="tpu_custom_call" | custom-call | flops 128 | bytes 128 | tf_op jit(solution)/shard_map/merge/pallas_call | solution.py:251
  86.7 25.5 %all_to_all.11 = bf16[64,24,128]{2,1,0:T(8,128)(2,1)S(1)} all-to-all(bf16[64,24,128]{2,1,0:T(8,128)(2,1)S(1)} %bitcast.29), channel_id=1, replica_groups=mesh['stretch'=4,'seq'=64] {'seq'}, dimensions={0} | all-to-all | bytes 786432 | tf_op jit(solution)/shard_map/all_to_all | solution.py:316
  112.2 0.1 copy.15
  112.2 0.9 reshape.27
  (4 shorter events, 0.1 us)
Async XLA Ops:
  49.7 17.7 %collective-permute-start = (bf16[2,1536,128]{2,1,0:T(8,128)(2,1)S(1)}, bf16[2,1536,128]{2,1,0:T(8,128)(2,1)S(1)}, u32[]{:S(2)}, u32[]{:S(2)}) collective-permute-start(bf16[2,1536,128]{2,1,0:T(8,128)(2,1)S(1)} %bitcast.25), channel_id=1, source_target_pairs={{0,16},{1,17},{2,18},{3,19},{4,20},{5,21},{6,22},{7,23},{8,24},{9,... | collective-permute-start | bytes 2359304 | tf_op jit(solution)/shard_map/ppermute | solution.py:32
  49.9 9.7 %collective-permute-start.1 = (bf16[1600,128]{1,0:T(8,128)(2,1)S(1)}, bf16[1600,128]{1,0:T(8,128)(2,1)S(1)}, u32[]{:S(2)}, u32[]{:S(2)}) collective-permute-start(bf16[1600,128]{1,0:T(8,128)(2,1)S(1)} %pad_maximum_fusion.1), channel_id=1, source_target_pairs={{128,0},{129,1},{130,2},{131,3},{132,4},{133,5},{134,6},{135,7},{1... | collective-permute-start | bytes 1228808 | tf_op jit(solution)/shard_map/ppermute | solution.py:32
  53.9 1.8 %collective-permute-start.2 = (bf16[1536,128]{1,0:T(8,128)(2,1)S(1)}, bf16[1536,128]{1,0:T(8,128)(2,1)S(1)}, u32[]{:S(2)}, u32[]{:S(2)}) collective-permute-start(bf16[1536,128]{1,0:T(8,128)(2,1)S(1)} %bitcast.38), channel_id=1, source_target_pairs={{0,64},{1,65},{2,66},{3,67},{4,68},{5,69},{6,70},{7,71},{8,72},{9,... | collective-permute-start | bytes 1179656 | tf_op jit(solution)/shard_map/ppermute | solution.py:32
  54.0 2.3 %collective-permute-start.3 = (bf16[1536,128]{1,0:T(8,128)(2,1)S(1)}, bf16[1536,128]{1,0:T(8,128)(2,1)S(1)}, u32[]{:S(2)}, u32[]{:S(2)}) collective-permute-start(bf16[1536,128]{1,0:T(8,128)(2,1)S(1)} %bitcast.37), channel_id=1, source_target_pairs={{0,64},{1,65},{2,66},{3,67},{4,68},{5,69},{6,70},{7,71},{8,72},{9,... | collective-permute-start | bytes 1179656 | tf_op jit(solution)/shard_map/ppermute | solution.py:32
  67.4 3.8 %collective-permute-start.4 = (bf16[2,1536,128]{2,1,0:T(8,128)(2,1)S(1)}, bf16[2,1536,128]{2,1,0:T(8,128)(2,1)S(1)}, u32[]{:S(2)}, u32[]{:S(2)}) collective-permute-start(bf16[2,1536,128]{2,1,0:T(8,128)(2,1)S(1)} %collective-permute-done.kv_ref), channel_id=1, source_target_pairs={{0,64},{1,65},{2,66},{3,67},{4,68},{5,69},{6,70},{7,71},{8,72},{9,... | collective-permute-start | bytes 2359304 | tf_op jit(solution)/shard_map/ppermute | solution.py:32
  71.3 10.2 %collective-permute-start.5 = (bf16[816,128]{1,0:T(8,128)(2,1)S(1)}, bf16[816,128]{1,0:T(8,128)(2,1)S(1)}, u32[]{:S(2)}, u32[]{:S(2)}) collective-permute-start(bf16[816,128]{1,0:T(8,128)(2,1)S(1)} %chip_far0.1), channel_id=1, source_target_pairs={{0,128},{1,129},{2,130},{3,131},{4,132},{5,133},{6,134},{7,135},{8... | collective-permute-start | bytes 626696 | tf_op jit(solution)/shard_map/ppermute | solution.py:32
  72.6 12.8 %copy-start = (f32[64,4096]{1,0:T(8,128)S(1)}, f32[64,4096]{1,0:T(8,128)}, u32[]{:S(2)}) copy-start(f32[64,4096]{1,0:T(8,128)} %gate_ref.1) | copy-start | bytes 3145732
  72.6 12.8 %copy-start.1 = (s32[4]{0:T(128)S(1)}, s32[4]{0:T(128)}, u32[]{:S(2)}) copy-start(s32[4]{0:T(128)} %levels_ref.1) | copy-start | bytes 52
  72.6 12.7 %collective-permute-start.6 = (bf16[816,128]{1,0:T(8,128)(2,1)S(1)}, bf16[816,128]{1,0:T(8,128)(2,1)S(1)}, u32[]{:S(2)}, u32[]{:S(2)}) collective-permute-start(bf16[816,128]{1,0:T(8,128)(2,1)S(1)} %chip_far1.1), channel_id=1, source_target_pairs={{0,128},{1,129},{2,130},{3,131},{4,132},{5,133},{6,134},{7,135},{8... | collective-permute-start | bytes 626696 | tf_op jit(solution)/shard_map/ppermute | solution.py:32

commit v7 on v5

--- a/solution.py
+++ b/solution.py
@@ -291,7 +291,7 @@
     chip, first_in = lend(0, chip_near)
     chip, chip_near = lax.optimization_barrier((chip, chip_near))
     chip, second_in = lend(1, chip_near)
-    first_in, chip, far = lax.optimization_barrier((first_in, chip, far))
+    chip, far = lax.optimization_barrier((chip, far))
     own = call(
         last_kernel, "last", [q, kv_x_core, far], [HELD] * 3, own_shape, [HELD] * 2, []
     )

time: 115 us -> 118 us (1.026)
  waiting for transfers between devices: 22.4 us -> 25.5 us
    ppermute x7, waiting for transfers between devices: 22.4 us -> 25.5 us  [send(): return lax.ppermute(array, AXES, pairs)]
where the time goes in v7:
time: 118 us; the launch traced here: 117 us
  blocking collectives  71.7 us (61%)
  waiting for transfers between devices  25.5 us (22%)
  Pallas kernels  9.2 us (8%)
  starting transfers between devices  7.45 us (6%)
  local copies, waits for them, and re-layouts  2.04 us (2%)
  other arithmetic  1.39 us (1%)
    all_to_all x1, blocking collectives, local(): qkv = lax.all_to_all(qkv, 'seq', 0, 0, tiled=True)  47.2 us
    ppermute x7, waiting for transfers between devices, send(): return lax.ppermute(array, AXES, pairs)  25.5 us
    all_to_all x1, blocking collectives, local(): lax.all_to_all(mixture.reshape(64, half, DH), 'seq', 0, 0, tiled=True)  24.5 us
    pallas_call x7, Pallas kernels, call(): pl.pallas_call(kernel, in_specs=in_specs, out_specs=out_spec, out_shape=o...  9.2 us
    ppermute x7, starting transfers between devices, send(): return lax.ppermute(array, AXES, pairs)  7.45 us
  transfers between devices with their start and end apart: 7, of which 5 were waited for; matrix products, arithmetic and copies ran while one was open for 0% of the time, Pallas kernels for 7%

profile of v7, /device:TPU:32, one launch (start us, length us, event | category | flops | bytes accessed | tf_op | source)
XLA Modules:
  0.0 117.5 jit_solution(11366077726634950696)
XLA Ops:
  0.0 1.4 %pad_maximum_fusion = bf16[3,48,4096]{2,1,0:T(8,128)(2,1)S(1)} fusion(bf16[1,48,4096]{2,1,0:T(8,128)(2,1)} %param.7, bf16[1,48,4096]{2,1,0:T(8,128)(2,1)} %param.6, bf16[1,48,4096]{2,1,0:T(8,128)(2,1)} %param.5), kind=kLoop, calls=%fused_computation | loop fusion | flops 1179648 | bytes 2359296 | tf_op jit(solution)/shard_map/concatenate | solution.py:258
  1.4 0.2 copy.12
  1.6 0.5 copy.9
  2.1 47.2 %all_to_all.10 = bf16[64,3,24,128]{3,2,1,0:T(8,128)(2,1)S(1)} all-to-all(bf16[64,3,24,128]{3,2,1,0:T(8,128)(2,1)S(1)} %bitcast.33), channel_id=1, replica_groups=mesh['stretch'=4,'seq'=64] {'seq'}, dimensions={0} | all-to-all | bytes 2359296 | tf_op jit(solution)/shard_map/all_to_all | solution.py:260
  49.3 0.1 slice.30
  49.4 0.2 fusion
  49.6 0.1 copy.10
  49.7 0.1 collective-permute-start
  49.9 4.0 %collective-permute-start.1 = (bf16[1600,128]{1,0:T(8,128)(2,1)S(1)}, bf16[1600,128]{1,0:T(8,128)(2,1)S(1)}, u32[]{:S(2)}, u32[]{:S(2)}) collective-permute-start(bf16[1600,128]{1,0:T(8,128)(2,1)S(1)} %pad_maximum_fusion.1), channel_id=1, source_target_pairs={{128,0},{129,1},{130,2},{131,3},{132,4},{133,5},{134,6},{135,7},{1... | collective-permute-start | bytes 1228808 | tf_op jit(solution)/shard_map/ppermute | solution.py:32
  53.9 0.1 collective-permute-start.2
  54.0 0.5 collective-permute-start.3
  54.5 1.2 %collective-permute-done.2.kc_ref = bf16[1536,128]{1,0:T(8,128)(2,1)S(1)} collective-permute-done((bf16[1536,128]{1,0:T(8,128)(2,1)S(1)}, bf16[1536,128]{1,0:T(8,128)(2,1)S(1)}, u32[]{:S(2)}, u32[]{:S(2)}) %collective-permute-start.2) | collective-permute-done | bytes 393248 | tf_op jit(solution)/shard_map/ppermute | solution.py:32
  55.7 0.6 collective-permute-done.3.vc_ref
  56.3 3.4 %near.1.before_ref = f32[3,1536,128]{2,1,0:T(8,128)S(1)} custom-call(bf16[1536,128]{1,0:T(8,128)(2,1)S(1)} %bitcast.22, bf16[2,1536,128]{2,1,0:T(8,128)(2,1)S(1)} %bitcast.27, bf16[1536,128]{1,0:T(8,128)(2,1)S(1)} %collective-permute-done.2.kc_ref, bf16[1536,128]{1,0:T(8,128)(2,1)S(1)} %collective-permute-done.3.vc_ref), custom_call_target="tpu_custom_call" | custom-call | flops 128 | bytes 128 | tf_op jit(solution)/shard_map/near/pallas_call | solution.py:241
  59.7 0.0 collective-permute-done.1.q_ref
  59.7 0.2 chip_near.1.near_ref
  59.9 7.6 %collective-permute-done.kv_ref = bf16[2,1536,128]{2,1,0:T(8,128)(2,1)S(1)} collective-permute-done((bf16[2,1536,128]{2,1,0:T(8,128)(2,1)S(1)}, bf16[2,1536,128]{2,1,0:T(8,128)(2,1)S(1)}, u32[]{:S(2)}, u32[]{:S(2)}) %collective-permute-start) | collective-permute-done | bytes 786464 | tf_op jit(solution)/shard_map/ppermute | solution.py:32
  67.4 0.0 collective-permute-start.4
  67.4 3.8 %far.1.before_ref = f32[3,1536,128]{2,1,0:T(8,128)S(1)} custom-call(bf16[1536,128]{1,0:T(8,128)(2,1)S(1)} %bitcast.23, bf16[2,1536,128]{2,1,0:T(8,128)(2,1)S(1)} %collective-permute-done.kv_ref, f32[3,1536,128]{2,1,0:T(8,128)S(1)} %near.1.before_ref), custom_call_target="tpu_custom_call", output_to_operand_aliasing={{}: (2, {})} | custom-call | flops 128 | bytes 128 | tf_op jit(solution)/shard_map/far/pallas_call | solution.py:241
  71.2 0.0 collective-permute-done.4.kvc_ref.kv_ref
  71.3 0.2 chip_far1.1
  71.5 0.0 copy-start
  71.5 0.0 copy-start.1
  71.5 1.4 %collective-permute-start.6 = (bf16[816,128]{1,0:T(8,128)(2,1)S(1)}, bf16[816,128]{1,0:T(8,128)(2,1)S(1)}, u32[]{:S(2)}, u32[]{:S(2)}) collective-permute-start(bf16[816,128]{1,0:T(8,128)(2,1)S(1)} %chip_far1.1), channel_id=1, source_target_pairs={{0,128},{1,129},{2,130},{3,131},{4,132},{5,133},{6,134},{7,135},{8... | collective-permute-start | bytes 626696 | tf_op jit(solution)/shard_map/ppermute | solution.py:32
  73.0 1.3 %collective-permute-start.5 = (bf16[816,128]{1,0:T(8,128)(2,1)S(1)}, bf16[816,128]{1,0:T(8,128)(2,1)S(1)}, u32[]{:S(2)}, u32[]{:S(2)}) collective-permute-start(bf16[816,128]{1,0:T(8,128)(2,1)S(1)} %chip_far0.1), channel_id=1, source_target_pairs={{0,128},{1,129},{2,130},{3,131},{4,132},{5,133},{6,134},{7,135},{8... | collective-permute-start | bytes 626696 | tf_op jit(solution)/shard_map/ppermute | solution.py:32
  74.3 0.3 last.1
  74.5 12.3 %collective-permute-done.6.refs_1_ = bf16[816,128]{1,0:T(8,128)(2,1)S(1)} collective-permute-done((bf16[816,128]{1,0:T(8,128)(2,1)S(1)}, bf16[816,128]{1,0:T(8,128)(2,1)S(1)}, u32[]{:S(2)}, u32[]{:S(2)}) %collective-permute-start.6) | collective-permute-done | bytes 208928 | tf_op jit(solution)/shard_map/ppermute | solution.py:32
  86.9 3.9 %collective-permute-done.5.refs_0_ = bf16[816,128]{1,0:T(8,128)(2,1)S(1)} collective-permute-done((bf16[816,128]{1,0:T(8,128)(2,1)S(1)}, bf16[816,128]{1,0:T(8,128)(2,1)S(1)}, u32[]{:S(2)}, u32[]{:S(2)}) %collective-permute-start.5) | collective-permute-done | bytes 208928 | tf_op jit(solution)/shard_map/ppermute | solution.py:32
  90.7 0.0 copy-done
  90.8 0.0 copy-done.1
  90.8 1.3 %merge.1 = bf16[1536,128]{1,0:T(8,128)(2,1)S(1)} custom-call(s32[4]{0:T(128)S(1)} %copy-done.1, f32[64,4096]{1,0:T(8,128)S(1)} %copy-done, f32[1536,128]{1,0:T(8,128)S(1)} %get-tuple-element.27.own_ref, f32[16,128]{1,0:T(8,128)S(1)} %get-tuple-element.28.level_ref, bf16[816,128]{1,0:T(8,128)(2,1)S(1)} %collective-permute-done.5.refs_0_, ...), custom_call_target="tpu_custom_call" | custom-call | flops 128 | bytes 128 | tf_op jit(solution)/shard_map/merge/pallas_call | solution.py:241
  92.1 24.5 %all_to_all.11 = bf16[64,24,128]{2,1,0:T(8,128)(2,1)S(1)} all-to-all(bf16[64,24,128]{2,1,0:T(8,128)(2,1)S(1)} %bitcast.29), channel_id=1, replica_groups=mesh['stretch'=4,'seq'=64] {'seq'}, dimensions={0} | all-to-all | bytes 786432 | tf_op jit(solution)/shard_map/all_to_all | solution.py:303
  116.5 0.1 copy.14
  116.6 0.9 reshape.27
  (3 shorter events, 0.0 us)
Async XLA Ops:
  49.7 17.7 %collective-permute-start = (bf16[2,1536,128]{2,1,0:T(8,128)(2,1)S(1)}, bf16[2,1536,128]{2,1,0:T(8,128)(2,1)S(1)}, u32[]{:S(2)}, u32[]{:S(2)}) collective-permute-start(bf16[2,1536,128]{2,1,0:T(8,128)(2,1)S(1)} %bitcast.25), channel_id=1, source_target_pairs={{0,16},{1,17},{2,18},{3,19},{4,20},{5,21},{6,22},{7,23},{8,24},{9,... | collective-permute-start | bytes 2359304 | tf_op jit(solution)/shard_map/ppermute | solution.py:32
  49.9 9.8 %collective-permute-start.1 = (bf16[1600,128]{1,0:T(8,128)(2,1)S(1)}, bf16[1600,128]{1,0:T(8,128)(2,1)S(1)}, u32[]{:S(2)}, u32[]{:S(2)}) collective-permute-start(bf16[1600,128]{1,0:T(8,128)(2,1)S(1)} %pad_maximum_fusion.1), channel_id=1, source_target_pairs={{128,0},{129,1},{130,2},{131,3},{132,4},{133,5},{134,6},{135,7},{1... | collective-permute-start | bytes 1228808 | tf_op jit(solution)/shard_map/ppermute | solution.py:32
  53.9 1.8 %collective-permute-start.2 = (bf16[1536,128]{1,0:T(8,128)(2,1)S(1)}, bf16[1536,128]{1,0:T(8,128)(2,1)S(1)}, u32[]{:S(2)}, u32[]{:S(2)}) collective-permute-start(bf16[1536,128]{1,0:T(8,128)(2,1)S(1)} %bitcast.38), channel_id=1, source_target_pairs={{0,64},{1,65},{2,66},{3,67},{4,68},{5,69},{6,70},{7,71},{8,72},{9,... | collective-permute-start | bytes 1179656 | tf_op jit(solution)/shard_map/ppermute | solution.py:32
  54.0 2.3 %collective-permute-start.3 = (bf16[1536,128]{1,0:T(8,128)(2,1)S(1)}, bf16[1536,128]{1,0:T(8,128)(2,1)S(1)}, u32[]{:S(2)}, u32[]{:S(2)}) collective-permute-start(bf16[1536,128]{1,0:T(8,128)(2,1)S(1)} %bitcast.37), channel_id=1, source_target_pairs={{0,64},{1,65},{2,66},{3,67},{4,68},{5,69},{6,70},{7,71},{8,72},{9,... | collective-permute-start | bytes 1179656 | tf_op jit(solution)/shard_map/ppermute | solution.py:32
  67.4 3.8 %collective-permute-start.4 = (bf16[2,1536,128]{2,1,0:T(8,128)(2,1)S(1)}, bf16[2,1536,128]{2,1,0:T(8,128)(2,1)S(1)}, u32[]{:S(2)}, u32[]{:S(2)}) collective-permute-start(bf16[2,1536,128]{2,1,0:T(8,128)(2,1)S(1)} %collective-permute-done.kv_ref), channel_id=1, source_target_pairs={{0,64},{1,65},{2,66},{3,67},{4,68},{5,69},{6,70},{7,71},{8,72},{9,... | collective-permute-start | bytes 2359304 | tf_op jit(solution)/shard_map/ppermute | solution.py:32
  71.5 19.2 %copy-start = (f32[64,4096]{1,0:T(8,128)S(1)}, f32[64,4096]{1,0:T(8,128)}, u32[]{:S(2)}) copy-start(f32[64,4096]{1,0:T(8,128)} %gate_ref.1) | copy-start | bytes 3145732
  71.5 19.2 %copy-start.1 = (s32[4]{0:T(128)S(1)}, s32[4]{0:T(128)}, u32[]{:S(2)}) copy-start(s32[4]{0:T(128)} %levels_ref.1) | copy-start | bytes 52
  71.5 15.3 %collective-permute-start.6 = (bf16[816,128]{1,0:T(8,128)(2,1)S(1)}, bf16[816,128]{1,0:T(8,128)(2,1)S(1)}, u32[]{:S(2)}, u32[]{:S(2)}) collective-permute-start(bf16[816,128]{1,0:T(8,128)(2,1)S(1)} %chip_far1.1), channel_id=1, source_target_pairs={{0,128},{1,129},{2,130},{3,131},{4,132},{5,133},{6,134},{7,135},{8... | collective-permute-start | bytes 626696 | tf_op jit(solution)/shard_map/ppermute | solution.py:32
  73.0 17.8 %collective-permute-start.5 = (bf16[816,128]{1,0:T(8,128)(2,1)S(1)}, bf16[816,128]{1,0:T(8,128)(2,1)S(1)}, u32[]{:S(2)}, u32[]{:S(2)}) collective-permute-start(bf16[816,128]{1,0:T(8,128)(2,1)S(1)} %chip_far0.1), channel_id=1, source_target_pairs={{0,128},{1,129},{2,130},{3,131},{4,132},{5,133},{6,134},{7,135},{8... | collective-permute-start | bytes 626696 | tf_op jit(solution)/shard_map/ppermute | solution.py:32
